TPU v7x, 128 devices: a whole 4x4x4 slice. The times are simulated.
128 devices in a mesh: px: 8 (over z, core), py: 16 (over x, y).
Axes of the slice: x: 4, y: 4, z: 4, core: 2. Of those that a mesh axis runs over, the one named last changes fastest.
Arguments:
- a_blocks: bfloat16 [12288, 27, 4096], P(('px', 'py')), may hold values from -1.5 to 1.5
- p_blocks: bfloat16 [12288, 4096], P(('px', 'py')), may hold values from -0.75 to 0.75
- a_source: int32 [12288, 27], P(('px', 'py')), may hold values from 0 to 1119, as said below
- send_list: int32 [128, 128, 8], P(('px', 'py')), may hold values from -1 to 95, as said below
- agg_local: int32 [12288], P(('px', 'py')), may hold values from 0 to 15, as said below
- coarse_slot: int32 [12288, 27], P(('px', 'py')), may hold values from 0 to 26
- coarse_target: int32 [2048], P(('px', 'py')), may hold values from 0 to 2047, as said below
Outputs:
- coarse: bfloat16 [2048, 27, 4096], P(('px', 'py'))
Inputs may be any that keep to these rules, and one draw needn't show every extreme that they name: `a_source`: column 0 of a row is the row itself. An entry of 96 or more names a slot received from device (entry - 96) // 8, slot (entry - 96) % 8, which that device fills; every filled slot is named by some entry of the receiving device. `send_list`: filled slots from one sender to one receiver come first; no device sends to itself; each device fills all 8 slots for the device after it in px+py order; row 95 is sent in every draw. `agg_local`: each of a device's 16 agglomerates holds exactly 6 of its elements. `coarse_target`: A permutation of the coarse rows; the rows formed on a device go to devices with the same px index; at most 2 go from one device to one device, and in every draw exactly 2 for each pair that is used.
All inputs are finite; a program needn't handle non-finite values.
Results may differ from a plain program's by a relative error of at most 0.0049.
Values may be sent and summed in bfloat16 or wider, within the bound.
A program may use at most 384 MiB of HBM per device.

v0:
```python
import jax
import jax.numpy as jnp
from jax import lax
from jax.sharding import PartitionSpec as P

S = 27
AGG = 6
CCAP = 2


def triple_blocks(a_blocks, p_blocks, columns, agg_local, coarse_slot):
    rows_here, per_row, flat_size = a_blocks.shape
    block_size = int(round(flat_size**0.5))
    coarse_here = rows_here // AGG
    a_split = a_blocks.reshape(rows_here, per_row, block_size, block_size)
    col_split = columns.reshape(rows_here, per_row, block_size, block_size)
    product = jnp.einsum(
        "gkij,gkjl->gkil", a_split, col_split, preferred_element_type=jnp.float32
    ).astype(jnp.bfloat16)
    slot_hot = (coarse_slot[:, :, None] == jnp.arange(S)[None, None, :]).astype(jnp.bfloat16)
    grouped = jnp.einsum(
        "gks,gkm->gsm",
        slot_hot,
        product.reshape(rows_here, per_row, flat_size),
        preferred_element_type=jnp.float32,
    )
    own_split = p_blocks.reshape(rows_here, block_size, block_size).astype(jnp.float32)
    projected = jnp.einsum(
        "gia,gsil->gasl",
        own_split,
        grouped.reshape(rows_here, S, block_size, block_size),
        precision=lax.Precision.HIGHEST,
    )
    agg_hot = (jnp.arange(coarse_here)[:, None] == agg_local[None, :]).astype(jnp.float32)
    summed = jnp.dot(
        agg_hot,
        projected.reshape(rows_here, block_size * S * block_size),
        precision=lax.Precision.HIGHEST,
        preferred_element_type=jnp.float32,
    )
    summed = summed.reshape(coarse_here, block_size, S, block_size).transpose(0, 2, 1, 3)
    return summed.reshape(coarse_here, S, flat_size).astype(jnp.bfloat16)


def body(a_blocks, p_blocks, a_source, send_list, agg_local, coarse_slot, coarse_target):
    rows_here, flat_size = p_blocks.shape
    peer_count = lax.axis_size(("px", "py"))
    slot_count = send_list.shape[2]
    wanted = send_list.reshape(peer_count, slot_count)
    picked = jnp.take(p_blocks, jnp.maximum(wanted, 0).reshape(-1), axis=0).reshape(
        peer_count, slot_count, flat_size
    )
    outgoing = jnp.where((wanted >= 0)[:, :, None], picked, jnp.zeros_like(picked))
    arrived = lax.all_to_all(outgoing, ("px", "py"), split_axis=0, concat_axis=0, tiled=True)
    extended = jnp.concatenate(
        [p_blocks, arrived.reshape(peer_count * slot_count, flat_size)], axis=0
    )
    columns = jnp.take(extended, a_source, axis=0)
    partial_value = triple_blocks(a_blocks, p_blocks, columns, agg_local, coarse_slot)
    coarse_here = partial_value.shape[0]
    peers_y = lax.axis_size("py")
    order_idx = jnp.arange(coarse_here)
    dest_column = coarse_target // coarse_here % peers_y
    same_dest = dest_column[:, None] == dest_column[None, :]
    earlier = order_idx[None, :] < order_idx[:, None]
    bucket_rank = jnp.sum((same_dest & earlier).astype(jnp.int32), axis=1)
    bucket_index = dest_column * CCAP + bucket_rank
    send_rows = (
        jnp.zeros((peers_y * CCAP, S, flat_size), jnp.bfloat16).at[bucket_index].set(partial_value)
    )
    send_rows = send_rows.reshape(peers_y, CCAP, S, flat_size)
    send_places = (
        jnp.full((peers_y * CCAP,), -1, jnp.int32).at[bucket_index].set(coarse_target % coarse_here)
    )
    received, places = (
        lax.all_to_all(send_rows, "py", split_axis=0, concat_axis=0, tiled=True),
        lax.all_to_all(
            send_places.reshape(peers_y, CCAP), "py", split_axis=0, concat_axis=0, tiled=True
        ),
    )
    landing = jnp.where(places >= 0, places, coarse_here).reshape(-1)
    coarse = (
        jnp.zeros((coarse_here, S, flat_size), jnp.bfloat16)
        .at[landing]
        .set(received.reshape(-1, S, flat_size), mode="drop")
    )
    return coarse


def solution(mesh):
    in_specs = (
        P(("px", "py"), None, None),
        P(("px", "py"), None),
        P(("px", "py"), None),
        P(("px", "py"), None, None),
        P(("px", "py")),
        P(("px", "py"), None),
        P(("px", "py")),
    )
    out_specs = P(("px", "py"), None, None)
    return jax.shard_map(body, mesh=mesh, in_specs=in_specs, out_specs=out_specs, check_vma=False)
```

profile of v0, /device:TPU:60, one launch (start us, length us, event | category | flops | bytes accessed | tf_op | source)
XLA Modules:
  0.0 1027.2 jit_solution(6613666073114522508)
XLA Ops:
  1.8 16.3 %gather_fusion = bf16[1024,4096]{1,0:T(8,128)(2,1)} fusion(bf16[96,4096]{1,0:T(8,128)(2,1)} %param.8, s32[1024]{0:T(1024)S(1)} %broadcast_clamp_fusion), kind=kCustom, calls=%fused_computation | custom fusion | bytes 16781312 | tf_op jit(solution)/shard_map/jit(_take)/gather | solution.py:50
  18.2 7.4 fusion.8
  25.6 10.5 %all-to-all-start.1 = ((bf16[128,8,4096]{2,1,0:T(8,128)(2,1)}), bf16[128,8,4096]{2,1,0:T(8,128)(2,1)}, u32[]{:S(2)}, u32[]{:S(2)}) async-start(bf16[128,8,4096]{2,1,0:T(8,128)(2,1)} %fusion.8), calls=%async_computation.1 | async-start | bytes 16777216 | tf_op jit(solution)/shard_map/all_to_all | solution.py:54
  37.1 31.9 %copy.85 = bf16[96,27,4096]{0,2,1:T(8,128)(2,1)} copy(bf16[96,27,4096]{2,0,1:T(8,128)(2,1)} %param.7) | data formatting | bytes 42467328 | tf_op args[0]
  69.0 66.5 %copy.87 = bf16[96,27,64,64]{3,2,1,0:T(8,128)(2,1)} copy(bf16[96,27,64,64]{0,3,2,1:T(8,128)(2,1)} %bitcast.50) | data formatting | bytes 42467328 | tf_op jit(solution)/shard_map/reshape | solution.py:15
  135.6 0.7 copy.79
  136.3 3.0 copy.102
  140.9 7.5 all-to-all-start
  148.4 8.3 pad_maximum_fusion
  156.7 43.1 %gather_fusion.1 = bf16[2592,4096]{1,0:T(8,128)(2,1)} fusion(bf16[1120,4096]{1,0:T(8,128)(2,1)} %pad_maximum_fusion, s32[3072]{0:T(1024)S(1)} %pad_clamp_fusion), kind=kCustom, calls=%fused_computation.1 | custom fusion | bytes 42477696 | tf_op jit(solution)/shard_map/jit(_take)/gather | solution.py:58
  199.8 56.9 %gather.15 = bf16[96,27,64,64]{3,2,1,0:T(8,128)(2,1)} reshape(bf16[2592,4096]{1,0:T(8,128)(2,1)} %gather_fusion.1) | data formatting | bytes 42467328 | tf_op jit(solution)/shard_map/jit(_take)/gather | solution.py:58
  256.6 49.6 %convert_bitcast_fusion = bf16[96,27,64,64]{2,3,1,0:T(8,128)(2,1)} fusion(bf16[96,27,64,64]{3,2,1,0:T(8,128)(2,1)} %copy.87, bf16[96,27,64,64]{3,2,1,0:T(8,128)(2,1)} %gather.15, pred[96,27]{1,0:T(8,128)(4,1)S(1)} %copy.80), kind=kOutput, calls=%fused_computation.7 | convolution fusion | flops 1380188160 | bytes 63703584 | tf_op jit(solution)/shard_map/gkij,gkjl->gkil/dot_general | solution.py:17
  306.2 73.5 %copy.88 = bf16[96,27,64,64]{0,3,2,1:T(8,128)(2,1)} copy(bf16[96,27,64,64]{2,3,1,0:T(8,128)(2,1)} %convert_bitcast_fusion) | data formatting | bytes 42467328 | tf_op jit(solution)/shard_map/convert_element_type | solution.py:19
  379.8 39.7 %copy.89 = bf16[96,27,4096]{2,1,0:T(8,128)(2,1)} copy(bf16[96,27,4096]{0,2,1:T(8,128)(2,1)} %bitcast.49) | data formatting | bytes 42467328 | tf_op jit(solution)/shard_map/reshape | solution.py:24
  419.5 24.9 %fusion.11 = f32[96,27,4096]{2,1,0:T(8,128)} fusion(bf16[96,27,4096]{2,1,0:T(8,128)(2,1)} %copy.89, s32[96,27]{1,0:T(8,128)S(1)} %copy-done.2), kind=kOutput, calls=%fused_computation.18 | convolution fusion | flops 573378944 | bytes 63711360 | tf_op jit(solution)/shard_map/gks,gkm->gsm/dot_general | solution.py:21
  444.4 54.1 %copy.90 = f32[96,27,4096]{0,2,1:T(8,128)} copy(f32[96,27,4096]{2,1,0:T(8,128)} %fusion.11) | data formatting | bytes 84934656 | tf_op jit(solution)/shard_map/gks,gkm->gsm/dot_general | solution.py:21
  498.4 85.4 %copy.92 = f32[96,27,64,64]{2,3,1,0:T(8,128)} copy(f32[96,27,64,64]{0,3,2,1:T(8,128)} %bitcast.48) | data formatting | bytes 84934656 | tf_op jit(solution)/shard_map/reshape | solution.py:31
  583.9 72.5 %convolution_bitcast_fusion = f32[96,64,27,64]{1,3,2,0:T(8,128)} fusion(f32[96,27,64,64]{2,3,1,0:T(8,128)} %copy.92, bf16[96,64,64,1]{2,1,3,0:T(8,128)(2,1)S(1)} %copy-done.1), kind=kOutput, calls=%fused_computation.11 | convolution fusion | flops 8153726976 | bytes 85721088 | tf_op jit(solution)/shard_map/gia,gsil->gasl/dot_general | solution.py:28
  656.4 83.4 %copy.94 = f32[96,64,27,64]{0,3,2,1:T(8,128)} copy(f32[96,64,27,64]{1,3,2,0:T(8,128)} %convolution_bitcast_fusion) | data formatting | bytes 84934656 | tf_op jit(solution)/shard_map/gia,gsil->gasl/dot_general | solution.py:28
  739.7 73.2 %convert_bitcast_fusion.1 = bf16[16,27,64,64]{3,0,1,2:T(8,128)(2,1)} fusion(f32[96,64,27,64]{0,3,2,1:T(8,128)} %copy.94, s32[96]{0:T(128)S(1)} %copy-done.5), kind=kOutput, calls=%fused_computation.16 | convolution fusion | flops 2040202752 | bytes 46006656 | tf_op jit(solution)/shard_map/dot_general | solution.py:35
  813.0 7.8 copy.106
  820.8 10.4 %reshape.168 = bf16[16,27,4096]{2,1,0:T(8,128)(2,1)} reshape(bf16[16,27,64,64]{3,2,1,0:T(8,128)(2,1)} %copy.106) | data formatting | bytes 7077888 | tf_op jit(solution)/shard_map/convert_element_type | solution.py:42
  831.1 4.3 broadcast_in_dim.64
  835.4 11.0 %scatter_fusion = bf16[32,27,4096]{2,1,0:T(8,128)(2,1)} fusion(bf16[32,27,4096]{2,1,0:T(8,128)(2,1)} %broadcast_in_dim.64, s32[16]{0:T(128)S(1)} %copy-done.7, bf16[16,27,4096]{2,1,0:T(8,128)(2,1)} %reshape.168), kind=kCustom, calls=%fused_computation.3 | custom fusion | bytes 10616896 | tf_op jit(solution)/shard_map/scatter | solution.py:69
  846.4 14.5 %copy.97 = bf16[16,2,27,4096]{3,1,2,0:T(2,128)(2,1)} copy(bf16[16,2,27,4096]{3,2,1,0:T(8,128)(2,1)} %bitcast.51) | data formatting | bytes 14155776 | tf_op jit(solution)/shard_map/reshape | solution.py:71
  860.9 7.3 all-to-all-start.2
  868.6 1.4 reduce.3
  870.1 118.2 %all-to-all-done.2 = bf16[16,2,27,4096]{3,1,2,0:T(2,128)(2,1)} async-done(((bf16[16,2,27,4096]{3,1,2,0:T(2,128)(2,1)}), bf16[16,2,27,4096]{3,1,2,0:T(2,128)(2,1)}, u32[]{:S(2)}, u32[]{:S(2)}) %all-to-all-start.2) | async-done | bytes 7077920 | tf_op jit(solution)/shard_map/all_to_all | solution.py:76
  988.3 11.7 %copy.107 = bf16[16,2,27,4096]{3,2,1,0:T(8,128)(2,1)} copy(bf16[16,2,27,4096]{3,1,2,0:T(2,128)(2,1)} %all-to-all-done.2) | data formatting | bytes 14155776 | tf_op jit(solution)/shard_map/reshape | solution.py:85
  1000.1 2.5 broadcast_in_dim.60
  1002.5 18.5 %scatter_fusion.1 = bf16[16,27,4096]{2,1,0:T(8,128)(2,1)} fusion(bf16[16,27,4096]{2,1,0:T(8,128)(2,1)} %broadcast_in_dim.60, s32[32]{0:T(128)S(1)} %fusion.18, bf16[32,27,4096]{2,1,0:T(8,128)(2,1)} %bitcast.52), kind=kCustom, calls=%fused_computation.4 | custom fusion | bytes 21233792 | tf_op jit(solution)/shard_map/scatter | solution.py:85
  1021.0 6.0 copy.100
  (42 shorter events, 5.0 us)
Async XLA Ops:
  25.6 10.5 %copy-start = (bf16[96,4096]{1,0:T(8,128)(2,1)S(1)}, bf16[96,4096]{1,0:T(8,128)(2,1)}, u32[]{:S(2)}) copy-start(bf16[96,4096]{1,0:T(8,128)(2,1)} %param.8) | copy-start | bytes 2359300
  25.6 11.2 %copy-start.3 = (s32[96,27]{0,1:T(8,128)S(1)}, s32[96,27]{0,1:T(8,128)}, u32[]{:S(2)}) copy-start(s32[96,27]{0,1:T(8,128)} %param.9) | copy-start | bytes 31108
  25.6 115.3 %all-to-all-start.1 = ((bf16[128,8,4096]{2,1,0:T(8,128)(2,1)}), bf16[128,8,4096]{2,1,0:T(8,128)(2,1)}, u32[]{:S(2)}, u32[]{:S(2)}) async-start(bf16[128,8,4096]{2,1,0:T(8,128)(2,1)} %fusion.8), calls=%async_computation.1 | async-start | bytes 16777216 | tf_op jit(solution)/shard_map/all_to_all | solution.py:54
  69.0 66.6 %copy-start.4 = (s32[96,27]{0,1:T(8,128)S(1)}, s32[96,27]{0,1:T(8,128)}, u32[]{:S(2)}) copy-start(s32[96,27]{0,1:T(8,128)} %param.12) | copy-start | bytes 31108
  69.0 70.4 %copy-start.8 = (s32[16]{0:T(128)S(1)}, s32[16]{0:T(128)}, u32[]{:S(2)}) copy-start(s32[16]{0:T(128)} %param.13) | copy-start | bytes 196
  139.6 17.1 %copy-start.6 = (s32[16]{0:T(128)}, s32[16]{0:T(128)S(1)}, u32[]{:S(2)}) copy-start(s32[16]{0:T(128)S(1)} %compare_select_fusion.3) | copy-start | bytes 196
  140.9 720.0 %all-to-all-start = ((s32[16,1,2]{2,1,0:T(1,128)}), s32[16,1,2]{2,1,0:T(1,128)}, u32[]{:S(2)}, u32[]{:S(2)}) async-start(s32[16,1,2]{2,1,0:T(1,128)} %bitcast), calls=%async_computation | async-start | bytes 16384 | tf_op jit(solution)/shard_map/all_to_all | solution.py:77
  379.8 39.7 %copy-start.2 = (s32[96,27]{1,0:T(8,128)S(1)}, s32[96,27]{1,0:T(8,128)}, u32[]{:S(2)}) copy-start(s32[96,27]{1,0:T(8,128)} %copy.79) | copy-start | bytes 31108
  498.4 85.4 %copy-start.1 = (bf16[96,64,64,1]{2,1,3,0:T(8,128)(2,1)S(1)}, bf16[96,64,64,1]{2,1,3,0:T(8,128)(2,1)}, u32[]{:S(2)}) copy-start(bf16[96,64,64,1]{2,1,3,0:T(8,128)(2,1)} %copy.102) | copy-start | bytes 2359300
  656.4 83.4 %copy-start.5 = (s32[96]{0:T(128)S(1)}, s32[96]{0:T(128)}, u32[]{:S(2)}) copy-start(s32[96]{0:T(128)} %param.11) | copy-start | bytes 1156
  820.8 14.6 %copy-start.7 = (s32[16]{0:T(128)S(1)}, s32[16]{0:T(128)}, u32[]{:S(2)}) copy-start(s32[16]{0:T(128)} %copy-done.6) | copy-start | bytes 196
  860.9 127.5 %all-to-all-start.2 = ((bf16[16,2,27,4096]{3,1,2,0:T(2,128)(2,1)}), bf16[16,2,27,4096]{3,1,2,0:T(2,128)(2,1)}, u32[]{:S(2)}, u32[]{:S(2)}) async-start(bf16[16,2,27,4096]{3,1,2,0:T(2,128)(2,1)} %copy.97), calls=%async_computation.2 | async-start | bytes 14155776 | tf_op jit(solution)/shard_map/all_to_all | solution.py:76
where the time goes:
time: 1050 us; the launch traced here: 1030 us
  local copies, waits for them, and re-layouts  644 us (61%)
  matrix products  220 us (21%)
  waiting for transfers between devices  118 us (11%)
  starting transfers between devices  25.3 us (2%)
  other arithmetic  18.7 us (2%)
    all_to_all x1, waiting for transfers between devices, body(): lax.all_to_all(send_rows, 'py', split_axis=0, concat_axis=0, tiled=True)  118 us
    gather x2, local copies, waits for them, and re-layouts, body(): columns = jnp.take(extended, a_source, axis=0)  100 us
    reshape x1, local copies, waits for them, and re-layouts, triple_blocks(): grouped.reshape(rows_here, S, block_size, block_size)  85.4 us
    dot_general x1, local copies, waits for them, and re-layouts, triple_blocks(): jnp.einsum('gia,gsil->gasl', own_split, grouped.reshape(rows_here, S, blo...  83.4 us
    convert_element_type x1, local copies, waits for them, and re-layouts, triple_blocks(): product = jnp.einsum('gkij,gkjl->gkil', a_split, col_split, preferred_ele...  73.5 us
    dot_general x1, matrix products, triple_blocks(): jnp.dot(agg_hot, projected.reshape(rows_here, block_size * S * block_size...  73.2 us
    dot_general x1, matrix products, triple_blocks(): jnp.einsum('gia,gsil->gasl', own_split, grouped.reshape(rows_here, S, blo...  72.5 us
    reshape x1, local copies, waits for them, and re-layouts, triple_blocks(): a_split = a_blocks.reshape(rows_here, per_row, block_size, block_size)  66.5 us
  transfers between devices with their start and end apart: 3, of which 1 were waited for; matrix products, arithmetic and copies ran while one was open for 80% of the time, Pallas kernels for 0%

commit v1 on v0

v1 whole, which is shorter than its diff:
```python
import jax
import jax.numpy as jnp
from jax import lax
from jax.experimental import pallas as pl
from jax.experimental.pallas import tpu as pltpu
from jax.sharding import PartitionSpec as P

B = 64
L = 2 * B
NB = 96
K = 27
S = 27
AGG = 6
Q = 8
CCAP = 2
NCL = NB // AGG
PEERS = 128
DEST = NCL * S
GROUP = 4
TILES = PEERS * Q // 2
LOCAL = NB + 2
GROUPS = 1024
POSITIONS = GROUPS * GROUP
CHUNK = 64
BATCH = 16
STEPS = GROUPS // CHUNK
ROWS_STEP = 16
F32 = jnp.float32
BF16 = jnp.bfloat16


def low_lanes(shape):
    return lax.broadcasted_iota(jnp.int32, shape, 1) < B


def params(limit):
    return pltpu.CompilerParams(
        dimension_semantics=("arbitrary",), vmem_limit_bytes=limit * 1024 * 1024
    )


def pack_kernel(wanted, p_ref, send_ref, local_ref, wide):
    step = pl.program_id(0)

    @pl.when(step == 0)
    def _():
        low = low_lanes((ROWS_STEP, L))

        def relayout(group, carry):
            row = pl.multiple_of(group * ROWS_STEP, ROWS_STEP)
            for m in range(B // 2):
                both = p_ref[pl.ds(row, ROWS_STEP), pl.ds(m * L, L)].astype(F32)
                turned = pltpu.roll(both, B, 1)
                even = jnp.where(low, both, turned)
                odd = jnp.where(low, turned, both)
                wide[pl.ds(2 * m, ROWS_STEP, stride=B), :] = even
                wide[pl.ds(2 * m + 1, ROWS_STEP, stride=B), :] = odd
            for g in range(ROWS_STEP):
                local_ref[row + g] = wide[pl.ds(g * B, B), :].astype(BF16)
            return carry

        lax.fori_loop(0, NB // ROWS_STEP, relayout, 0)
        zero = jnp.zeros((B, L), BF16)
        local_ref[NB] = zero
        local_ref[NB + 1] = zero

    low = low_lanes((B, L))
    per_step = send_ref.shape[0]

    def fill(tile, carry):
        slot = 2 * (step * per_step + tile)
        first = wanted[slot]
        second = wanted[slot + 1]
        first = jnp.where(first < 0, NB, first)
        second = jnp.where(second < 0, NB, second)
        send_ref[tile] = jnp.where(low, local_ref[first], local_ref[second])
        return carry

    lax.fori_loop(0, per_step, fill, 0, unroll=8)


def pack(wanted, p_blocks):
    per_step = TILES // 8
    return pl.pallas_call(
        pack_kernel,
        grid_spec=pltpu.PrefetchScalarGridSpec(
            num_scalar_prefetch=1,
            grid=(TILES // per_step,),
            in_specs=[pl.BlockSpec((NB, B * B), lambda i, w: (0, 0))],
            out_specs=[
                pl.BlockSpec((per_step, B, L), lambda i, w: (i, 0, 0)),
                pl.BlockSpec((LOCAL, B, L), lambda i, w: (0, 0, 0)),
            ],
            scratch_shapes=[pltpu.VMEM((ROWS_STEP * B, L), F32)],
        ),
        out_shape=[
            jax.ShapeDtypeStruct((TILES, B, L), BF16),
            jax.ShapeDtypeStruct((LOCAL, B, L), BF16),
        ],
        compiler_params=params(24),
        name="pack",
    )(wanted, p_blocks)


def left_kernel(
    dest_in, code_in, a_ref, p_ref, sorted_hbm, code_ref, group_ref, count_ref,
    held, wide, turned_p, cursor, sem,
):
    step = pl.program_id(0)

    @pl.when(step == 0)
    def _():
        def clear(d, carry):
            cursor[d] = 0
            return carry

        lax.fori_loop(0, DEST, clear, 0, unroll=8)

        def count(e, carry):
            d = dest_in[e]
            cursor[d] = cursor[d] + 1
            return carry

        lax.fori_loop(0, NB * K, count, 0, unroll=8)

        def place(d, at):
            here = cursor[d]
            cursor[d] = at
            return at + ((here + GROUP - 1) // GROUP) * GROUP

        total = lax.fori_loop(0, DEST, place, 0, unroll=8)
        count_ref[0] = total // GROUP

        def blank(i, carry):
            code_ref[i] = 2 * NB
            return carry

        lax.fori_loop(0, POSITIONS, blank, 0, unroll=16)

        def nowhere(i, carry):
            group_ref[i] = DEST
            return carry

        lax.fori_loop(0, GROUPS, nowhere, 0, unroll=16)
        zero = jnp.zeros((B, L), BF16)

        def wipe(i, carry):
            held[i] = zero
            return carry

        lax.fori_loop(0, 2 * GROUPS, wipe, 0, unroll=16)

    for g in range(ROWS_STEP):
        turned_p[g] = p_ref[g].astype(F32).T[:B].astype(BF16)

    low16 = low_lanes((ROWS_STEP, L))
    lane = lax.broadcasted_iota(jnp.int32, (B, L), 1)
    low = lane < B
    half = jnp.where(low, 0, 1)

    def insert(row, k, value, valid):
        e = (step * ROWS_STEP + row) * K + k
        d = dest_in[e]
        at = cursor[d]
        cursor[d] = at + valid
        at = jnp.where(valid == 1, at, POSITIONS)
        code_ref[at] = code_in[e]
        group_ref[at // GROUP] = d
        tile = at // 2
        held[tile] = jnp.where(half == at % 2, value, held[tile].astype(F32)).astype(BF16)

    def pair_step(pair, carry):
        first = 2 * pair
        valid = jnp.where(first + 1 < K, 1, 0)
        second = jnp.minimum(first + 1, K - 1)
        for m in range(B // 2):
            one = a_ref[first, :, pl.ds(m * L, L)].astype(F32)
            two = a_ref[second, :, pl.ds(m * L, L)].astype(F32)
            wide[pl.ds(2 * m, ROWS_STEP, stride=B), :] = jnp.where(
                low16, one, pltpu.roll(two, B, 1)
            )
            wide[pl.ds(2 * m + 1, ROWS_STEP, stride=B), :] = jnp.where(
                low16, pltpu.roll(one, B, 1), two
            )
        for row in range(ROWS_STEP):
            block = wide[pl.ds(row * B, B), :].astype(BF16)
            value = jnp.dot(turned_p[row], block, preferred_element_type=F32)
            turned = pltpu.roll(value, B, 1)
            insert(row, first, jnp.where(low, value, turned), 1)
            insert(row, second, jnp.where(low, turned, value), valid)
        return carry

    lax.fori_loop(0, (K + 1) // 2, pair_step, 0)

    @pl.when(step == pl.num_programs(0) - 1)
    def _():
        copy = pltpu.make_async_copy(held.at[pl.ds(0, 2 * GROUPS)], sorted_hbm, sem)
        copy.start()
        copy.wait()


def left(dest, code, a_turned, local):
    return pl.pallas_call(
        left_kernel,
        grid_spec=pltpu.PrefetchScalarGridSpec(
            num_scalar_prefetch=2,
            grid=(NB // ROWS_STEP,),
            in_specs=[
                pl.BlockSpec((K, ROWS_STEP, B * B), lambda i, *_: (0, i, 0)),
                pl.BlockSpec((ROWS_STEP, B, L), lambda i, *_: (i, 0, 0)),
            ],
            out_specs=[
                pl.BlockSpec(memory_space=pl.ANY),
                pl.BlockSpec(memory_space=pltpu.SMEM),
                pl.BlockSpec(memory_space=pltpu.SMEM),
                pl.BlockSpec(memory_space=pltpu.SMEM),
            ],
            scratch_shapes=[
                pltpu.VMEM((2 * GROUPS + 1, B, L), BF16),
                pltpu.VMEM((ROWS_STEP * B, L), F32),
                pltpu.VMEM((ROWS_STEP, B, B), BF16),
                pltpu.SMEM((DEST,), jnp.int32),
                pltpu.SemaphoreType.DMA,
            ],
        ),
        out_shape=[
            jax.ShapeDtypeStruct((2 * GROUPS, B, L), BF16),
            jax.ShapeDtypeStruct((POSITIONS + GROUP,), jnp.int32),
            jax.ShapeDtypeStruct((GROUPS + 1,), jnp.int32),
            jax.ShapeDtypeStruct((1,), jnp.int32),
        ],
        compiler_params=params(56),
        cost_estimate=pl.CostEstimate(
            flops=2 * NB * K * B**3 * 16, bytes_accessed=60_000_000, transcendentals=0
        ),
        name="left",
    )(dest, code, a_turned, local)


def right_kernel(
    code_ref, group_ref, count_ref, bucket_ref, t_ref, local_hbm, ghost_hbm, out_ref,
    blocks, total, wide, halves, sems,
):
    step = pl.program_id(0)
    groups = count_ref[0]

    @pl.when(step == 0)
    def _():
        mine = pltpu.make_async_copy(local_hbm, blocks.at[pl.ds(0, LOCAL)], sems.at[0])
        others = pltpu.make_async_copy(ghost_hbm, blocks.at[pl.ds(LOCAL, TILES)], sems.at[1])
        mine.start()
        others.start()
        low = low_lanes((B, L))
        halves[0] = jnp.where(low, 1.0, 0.0).astype(BF16)
        halves[1] = jnp.where(low, 0.0, 1.0).astype(BF16)
        zero = jnp.zeros((B, L), F32)

        def clear(i, carry):
            total[i] = zero
            return carry

        lax.fori_loop(0, DEST + 1, clear, 0, unroll=8)
        mine.wait()
        others.wait()

    @pl.when(step < STEPS)
    def _():
        def batch(b, carry):
            for u in range(BATCH):
                here = b * BATCH + u
                group = step * CHUNK + here
                lhs = jnp.concatenate([t_ref[2 * here], t_ref[2 * here + 1]], axis=1)
                parts = []
                for w in range(GROUP):
                    code = code_ref[group * GROUP + w]
                    parts.append(blocks[code // 2] * halves[code % 2])
                rhs = jnp.concatenate(parts, axis=0)
                d = group_ref[group]
                total[d] += jnp.dot(lhs, rhs, preferred_element_type=F32)
            return carry

        left_over = groups - step * CHUNK
        batches = jnp.clip((left_over + BATCH - 1) // BATCH, 0, CHUNK // BATCH)
        lax.fori_loop(0, batches, batch, 0)

    @pl.when(step >= STEPS)
    def _():
        base = (step - STEPS) * S
        low = low_lanes((B // 2, L))

        def emit(part, carry):
            for u in range(9):
                s = part * 9 + u
                value = total[base + s]
                wide[pl.ds(u * B, B), :] = value + pltpu.roll(value, B, 1)
                even = wide[pl.ds(u * B, B // 2, stride=2), :]
                odd = wide[pl.ds(u * B + 1, B // 2, stride=2), :]
                out_ref[0, s] = jnp.where(low, even, odd).astype(BF16)
            return carry

        lax.fori_loop(0, S // 9, emit, 0)


def right(code, group, count, bucket, ordered, local, ghost, peers_y):
    last = STEPS - 1

    def t_map(i, code_ref, group_ref, count_ref, bucket_ref):
        used = jnp.maximum((count_ref[0] + CHUNK - 1) // CHUNK - 1, 0)
        return (jnp.minimum(jnp.minimum(i, last), used), 0, 0)

    def out_map(i, code_ref, group_ref, count_ref, bucket_ref):
        return (bucket_ref[jnp.maximum(i - STEPS, 0)], 0, 0, 0)

    return pl.pallas_call(
        right_kernel,
        grid_spec=pltpu.PrefetchScalarGridSpec(
            num_scalar_prefetch=4,
            grid=(STEPS + NCL,),
            in_specs=[
                pl.BlockSpec((2 * CHUNK, B, L), t_map),
                pl.BlockSpec(memory_space=pl.ANY),
                pl.BlockSpec(memory_space=pl.ANY),
            ],
            out_specs=pl.BlockSpec((1, S, B // 2, L), out_map),
            scratch_shapes=[
                pltpu.VMEM((LOCAL + TILES, B, L), BF16),
                pltpu.VMEM((DEST + 1, B, L), F32),
                pltpu.VMEM((9 * B, L), F32),
                pltpu.VMEM((2, B, L), BF16),
                pltpu.SemaphoreType.DMA((2,)),
            ],
        ),
        out_shape=jax.ShapeDtypeStruct((peers_y * CCAP, S, B // 2, L), BF16),
        compiler_params=params(48),
        name="right",
    )(code, group, count, bucket, ordered, local, ghost)


def place_kernel(from_ref, in_ref, out_ref, wide):
    step = pl.program_id(0)
    span = NCL * B // 2

    @pl.when(step < NCL)
    def _():
        for s in range(S):
            wide[pl.ds(s * span + step, B // 2, stride=NCL), :] = in_ref[0, s].astype(F32)

    @pl.when(step >= NCL)
    def _():
        def flatten(u, carry):
            start = pl.multiple_of(((step - NCL) * 9 + u) * span, span)
            for m in range(B // 2):
                out_ref[u, :, pl.ds(m * L, L)] = wide[
                    pl.ds(start + m * NCL, NCL), :
                ].astype(BF16)
            return carry

        lax.fori_loop(0, 9, flatten, 0)


def place(origin, arrived):
    return pl.pallas_call(
        place_kernel,
        grid_spec=pltpu.PrefetchScalarGridSpec(
            num_scalar_prefetch=1,
            grid=(NCL + S // 9,),
            in_specs=[
                pl.BlockSpec(
                    (1, S, B // 2, L), lambda i, o: (o[jnp.minimum(i, NCL - 1)], 0, 0, 0)
                )
            ],
            out_specs=pl.BlockSpec((9, NCL, B * B), lambda i, o: (jnp.maximum(i - NCL, 0), 0, 0)),
            scratch_shapes=[pltpu.VMEM((S * NCL * B // 2, L), F32)],
        ),
        out_shape=jax.ShapeDtypeStruct((S, NCL, B * B), BF16),
        compiler_params=params(32),
        name="place",
    )(origin, arrived)


def lists(a_source, agg_local, coarse_slot):
    dest = (agg_local[:, None] * S + coarse_slot).reshape(-1)
    ghost = a_source - NB + 2 * LOCAL
    code = jnp.where(a_source < NB, 2 * a_source, ghost).reshape(-1)
    return dest, code


def routes(targets, me):
    column = targets // NCL % targets.shape[0]
    order = jnp.arange(NCL)
    same = column[:, :, None] == column[:, None, :]
    earlier = order[None, None, :] < order[None, :, None]
    rank = jnp.sum((same & earlier).astype(jnp.int32), axis=2)
    source = jnp.arange(targets.shape[0])[:, None] * CCAP + rank
    here = (column == me)[:, :, None] & ((targets % NCL)[:, :, None] == order[None, None, :])
    origin = jnp.sum(jnp.where(here, source[:, :, None], 0), axis=(0, 1))
    bucket = (column * CCAP + rank)[me]
    return bucket.astype(jnp.int32), origin.astype(jnp.int32)


def body(a_blocks, p_blocks, a_source, send_list, agg_local, coarse_slot, coarse_target):
    peers_y = lax.axis_size("py")
    me = lax.axis_index("py")
    sending, local = pack(send_list.reshape(-1), p_blocks)
    ghost = lax.all_to_all(
        sending.reshape(PEERS, Q // 2 * B, L), ("px", "py"), split_axis=0, concat_axis=0, tiled=True
    ).reshape(TILES, B, L)
    targets = lax.all_gather(coarse_target, "py")
    bucket, origin = routes(targets, me)
    dest, code = lists(a_source, agg_local, coarse_slot)
    ordered, code, group, count = left(dest, code, a_blocks.transpose(1, 0, 2), local)
    rows = right(code, group, count, bucket, ordered, local, ghost, peers_y)
    arrived = lax.all_to_all(
        rows.reshape(peers_y, CCAP * S * B // 2, L), "py", split_axis=0, concat_axis=0, tiled=True
    ).reshape(peers_y * CCAP, S, B // 2, L)
    return place(origin, arrived).transpose(1, 0, 2)


def solution(mesh):
    both = ("px", "py")
    in_specs = (
        P(both, None, None), P(both, None), P(both, None), P(both, None, None), P(both),
        P(both, None), P(both),
    )
    return jax.shard_map(
        body, mesh=mesh, in_specs=in_specs, out_specs=P(both, None, None), check_vma=False
    )
```

time: 1050 us -> 425 us (0.40)
  the two profiles are of different devices: /device:TPU:60 before, /device:TPU:116 now
where the time goes in v1:
time: 425 us; the launch traced here: 424 us
  Pallas kernels  181 us (43%)
  waiting for transfers between devices  110 us (26%)
  blocking collectives  103 us (24%)
  starting transfers between devices  18.6 us (4%)
  local copies, waits for them, and re-layouts  10.5 us (2%)
    all_to_all x1, waiting for transfers between devices, body(): lax.all_to_all(rows.reshape(peers_y, CCAP * S * B // 2, L), 'py', split_a...  110 us
    pallas_call x1, Pallas kernels, left(): pl.pallas_call(left_kernel, grid_spec=pltpu.PrefetchScalarGridSpec(num_sc...  109 us
    unnamed x1, blocking collectives  103 us
    pallas_call x1, Pallas kernels, right(): pl.pallas_call(right_kernel, grid_spec=pltpu.PrefetchScalarGridSpec(num_s...  51.5 us
    pallas_call x1, Pallas kernels, place(): pl.pallas_call(place_kernel, grid_spec=pltpu.PrefetchScalarGridSpec(num_s...  13 us
    all_to_all x1, starting transfers between devices, body(): lax.all_to_all(sending.reshape(PEERS, Q // 2 * B, L), ('px', 'py'), split...  10.2 us
    unnamed x26, local copies, waits for them, and re-layouts  8.6 us
  transfers between devices with their start and end apart: 2, of which 1 were waited for; matrix products, arithmetic and copies ran while one was open for 1% of the time, Pallas kernels for 26%

profile of v1, /device:TPU:116, one launch (start us, length us, event | category | flops | bytes accessed | tf_op | source)
XLA Modules:
  0.0 424.2 jit_solution(15010739098539337696)
XLA Ops:
  0.0 0.8 copy.13
  0.8 0.1 reshape.62.wanted
  0.9 0.0 copy-start.3
  0.9 1.1 copy-done.3
  2.0 7.2 %pack.1 = (bf16[512,64,128]{2,1,0:T(8,128)(2,1)S(1)}, bf16[98,64,128]{2,1,0:T(8,128)(2,1)S(1)}) custom-call(s32[1024]{0:T(1024)S(1)} %reshape.62.wanted, bf16[96,4096]{1,0:T(8,128)(2,1)S(1)} %copy-done.3), custom_call_target="tpu_custom_call" | custom-call | tf_op jit(solution)/shard_map/pack/pallas_call | solution.py:84
  9.2 0.0 copy-start
  9.2 3.2 copy-done
  12.4 1.2 copy-done.1
  13.6 0.0 copy-start.7
  13.6 10.2 %all-to-all-start = ((bf16[128,256,128]{2,1,0:T(8,128)(2,1)}), bf16[128,256,128]{2,1,0:T(8,128)(2,1)}, u32[]{:S(2)}, u32[]{:S(2)}) async-start(bf16[128,256,128]{2,1,0:T(8,128)(2,1)} %bitcast.9), calls=%async_computation | async-start | bytes 16777216 | tf_op jit(solution)/shard_map/all_to_all | solution.py:405
  23.8 0.0 copy-done.10
  23.8 0.6 dynamic-slice
  25.1 0.0 copy-done.8
  25.1 0.2 dynamic-update-slice
  25.3 102.9 %all-reduce = s32[256]{0:T(256)S(1)} all-reduce(s32[256]{0:T(256)S(1)} %dynamic-update-slice), channel_id=2, replica_groups=mesh['px'=8,'py'=16] {'py'}, use_global_device_ids=true, to_apply=%add | all-reduce | flops 256 | bytes 2048
  128.3 0.1 reshape.67
  128.3 0.1 copy.12
  128.4 0.8 reshape.61.code_in
  129.2 0.1 copy.11
  129.3 0.8 reshape.60.dest_in
  130.1 0.4 convert_reduce_fusion
  130.6 0.0 copy-start.2
  130.6 109.3 %left.1 = (bf16[2048,64,128]{2,1,0:T(8,128)(2,1)}, s32[4100]{0:T(1024)}, s32[1025]{0:T(1024)}, s32[1]{0:T(128)}) custom-call(s32[2592]{0:T(1024)} %reshape.60.dest_in, s32[2592]{0:T(1024)} %reshape.61.code_in, bf16[27,96,4096]{2,1,0:T(8,128)(2,1)} %bitcast.11, bf16[98,64,128]{2,1,0:T(8,128)(2,1)} %copy-done.1), custom_call_target="tpu_custom_call" | custom-call | flops 21743271936 | bytes 60000000 | tf_op jit(solution)/shard_map/left/pallas_call | solution.py:203
  239.9 0.0 all-to-all-done
  240.0 0.7 copy-done.4
  240.7 0.7 copy-done.5
  241.4 51.5 %right.1 = bf16[32,27,32,128]{3,2,1,0:T(8,128)(2,1)} custom-call(s32[4100]{0:T(1024)S(1)} %copy-done.4, s32[1025]{0:T(1024)S(1)} %copy-done.5, s32[1]{0:T(128)} %get-tuple-element.14.count_ref, s32[16]{0:T(128)S(1)} %fusion.4.bucket_ref, bf16[2048,64,128]{2,1,0:T(8,128)(2,1)} %get-tuple-element.15.t_ref, bf16[98,64,128]{2,1,0:T(8,128)(2,1)S(1)} %copy-done.2, ...), custom_call_target="tpu_custom_call" | custom-call | tf_op jit(solution)/shard_map/right/pallas_call | solution.py:314
  292.9 8.4 %all-to-all-start.1 = ((bf16[16,1728,128]{2,1,0:T(8,128)(2,1)}), bf16[16,1728,128]{2,1,0:T(8,128)(2,1)}, u32[]{:S(2)}, u32[]{:S(2)}) async-start(bf16[16,1728,128]{2,1,0:T(8,128)(2,1)} %bitcast.10), calls=%async_computation.1 | async-start | bytes 14155776 | tf_op jit(solution)/shard_map/all_to_all | solution.py:413
  301.3 0.1 broadcast_add_fusion.1
  301.4 0.2 select_reduce_fusion.from_ref
  301.6 109.7 %all-to-all-done.1 = bf16[16,1728,128]{2,1,0:T(8,128)(2,1)} async-done(((bf16[16,1728,128]{2,1,0:T(8,128)(2,1)}), bf16[16,1728,128]{2,1,0:T(8,128)(2,1)}, u32[]{:S(2)}, u32[]{:S(2)}) %all-to-all-start.1) | async-done | bytes 7077920 | tf_op jit(solution)/shard_map/all_to_all | solution.py:413
  411.2 13.0 %place.1 = bf16[27,16,4096]{2,1,0:T(8,128)(2,1)} custom-call(s32[16]{0:T(128)S(1)} %select_reduce_fusion.from_ref, bf16[32,27,32,128]{3,2,1,0:T(8,128)(2,1)} %bitcast.6.in_ref), custom_call_target="tpu_custom_call" | custom-call | tf_op jit(solution)/shard_map/place/pallas_call | solution.py:362
  (19 shorter events, 0.1 us)
Async XLA Ops:
  0.9 1.1 copy-start.3
  9.2 3.2 copy-start
  12.4 1.2 copy-start.1
  13.6 10.2 %copy-start.10 = (u32[128]{0:T(128)S(1)}, u32[128]{0:T(128)}, u32[]{:S(2)}) copy-start(u32[128]{0:T(128)} %constant.59) | copy-start | bytes 1540
  13.6 11.5 %copy-start.8 = (s32[16]{0:T(128)S(1)}, s32[16]{0:T(128)}, u32[]{:S(2)}) copy-start(s32[16]{0:T(128)} %param.13) | copy-start | bytes 196
  13.6 114.8 %copy-start.6 = (s32[96,27]{0,1:T(8,128)S(1)}, s32[96,27]{0,1:T(8,128)}, u32[]{:S(2)}) copy-start(s32[96,27]{0,1:T(8,128)} %param.9) | copy-start | bytes 31108
  13.6 115.7 %copy-start.9 = (s32[96]{0:T(128)S(1)}, s32[96]{0:T(128)}, u32[]{:S(2)}) copy-start(s32[96]{0:T(128)} %param.11) | copy-start | bytes 1156
  13.6 115.7 %copy-start.7 = (s32[96,27]{0,1:T(8,128)S(1)}, s32[96,27]{0,1:T(8,128)}, u32[]{:S(2)}) copy-start(s32[96,27]{0,1:T(8,128)} %param.12) | copy-start | bytes 31108
  13.6 226.4 %all-to-all-start = ((bf16[128,256,128]{2,1,0:T(8,128)(2,1)}), bf16[128,256,128]{2,1,0:T(8,128)(2,1)}, u32[]{:S(2)}, u32[]{:S(2)}) async-start(bf16[128,256,128]{2,1,0:T(8,128)(2,1)} %bitcast.9), calls=%async_computation | async-start | bytes 16777216 | tf_op jit(solution)/shard_map/all_to_all | solution.py:405
  130.6 109.4 %copy-start.2 = (bf16[98,64,128]{2,1,0:T(8,128)(2,1)S(1)}, bf16[98,64,128]{2,1,0:T(8,128)(2,1)}, u32[]{:S(2)}) copy-start(bf16[98,64,128]{2,1,0:T(8,128)(2,1)} %copy-done.1) | copy-start | bytes 4816900
  240.0 0.7 copy-start.4
  240.7 0.7 copy-start.5
  292.9 118.3 %all-to-all-start.1 = ((bf16[16,1728,128]{2,1,0:T(8,128)(2,1)}), bf16[16,1728,128]{2,1,0:T(8,128)(2,1)}, u32[]{:S(2)}, u32[]{:S(2)}) async-start(bf16[16,1728,128]{2,1,0:T(8,128)(2,1)} %bitcast.10), calls=%async_computation.1 | async-start | bytes 14155776 | tf_op jit(solution)/shard_map/all_to_all | solution.py:413

commit v2 on v1

--- a/solution.py
+++ b/solution.py
@@ -21,7 +21,10 @@
 LOCAL = NB + 2
 GROUPS = 1024
 POSITIONS = GROUPS * GROUP
-CHUNK = 64
+CHUNK = 128
+PITCH = 72
+SPAN = Q // 2 * B
+NOTE = 8
 BATCH = 16
 STEPS = GROUPS // CHUNK
 ROWS_STEP = 16
@@ -39,7 +42,7 @@
     )
 
 
-def pack_kernel(wanted, p_ref, send_ref, local_ref, wide):
+def pack_kernel(wanted, p_ref, note_ref, send_ref, local_ref, wide):
     step = pl.program_id(0)
 
     @pl.when(step == 0)
@@ -53,10 +56,10 @@
                 turned = pltpu.roll(both, B, 1)
                 even = jnp.where(low, both, turned)
                 odd = jnp.where(low, turned, both)
-                wide[pl.ds(2 * m, ROWS_STEP, stride=B), :] = even
-                wide[pl.ds(2 * m + 1, ROWS_STEP, stride=B), :] = odd
+                wide[pl.ds(2 * m, ROWS_STEP, stride=PITCH), :] = even
+                wide[pl.ds(2 * m + 1, ROWS_STEP, stride=PITCH), :] = odd
             for g in range(ROWS_STEP):
-                local_ref[row + g] = wide[pl.ds(g * B, B), :].astype(BF16)
+                local_ref[row + g] = wide[pl.ds(g * PITCH, B), :].astype(BF16)
             return carry
 
         lax.fori_loop(0, NB // ROWS_STEP, relayout, 0)
@@ -67,39 +70,46 @@
     low = low_lanes((B, L))
     per_step = send_ref.shape[0]
 
-    def fill(tile, carry):
-        slot = 2 * (step * per_step + tile)
-        first = wanted[slot]
-        second = wanted[slot + 1]
-        first = jnp.where(first < 0, NB, first)
-        second = jnp.where(second < 0, NB, second)
-        send_ref[tile] = jnp.where(low, local_ref[first], local_ref[second])
+    def fill(peer, carry):
+        for u in range(Q // 2):
+            slot = (step * per_step + peer) * Q + 2 * u
+            first = wanted[slot]
+            second = wanted[slot + 1]
+            first = jnp.where(first < 0, NB, first)
+            second = jnp.where(second < 0, NB, second)
+            send_ref[peer, u * B : (u + 1) * B] = jnp.where(
+                low, local_ref[first], local_ref[second]
+            )
+        send_ref[peer, SPAN:] = note_ref[...]
         return carry
 
-    lax.fori_loop(0, per_step, fill, 0, unroll=8)
-
-
-def pack(wanted, p_blocks):
-    per_step = TILES // 8
+    lax.fori_loop(0, per_step, fill, 0, unroll=2)
+
+
+def pack(wanted, p_blocks, note):
+    per_step = PEERS // 8
     return pl.pallas_call(
         pack_kernel,
         grid_spec=pltpu.PrefetchScalarGridSpec(
             num_scalar_prefetch=1,
-            grid=(TILES // per_step,),
-            in_specs=[pl.BlockSpec((NB, B * B), lambda i, w: (0, 0))],
+            grid=(PEERS // per_step,),
+            in_specs=[
+                pl.BlockSpec((NB, B * B), lambda i, w: (0, 0)),
+                pl.BlockSpec((NOTE, L), lambda i, w: (0, 0)),
+            ],
             out_specs=[
-                pl.BlockSpec((per_step, B, L), lambda i, w: (i, 0, 0)),
+                pl.BlockSpec((per_step, SPAN + NOTE, L), lambda i, w: (i, 0, 0)),
                 pl.BlockSpec((LOCAL, B, L), lambda i, w: (0, 0, 0)),
             ],
-            scratch_shapes=[pltpu.VMEM((ROWS_STEP * B, L), F32)],
+            scratch_shapes=[pltpu.VMEM((ROWS_STEP * PITCH, L), F32)],
         ),
         out_shape=[
-            jax.ShapeDtypeStruct((TILES, B, L), BF16),
+            jax.ShapeDtypeStruct((PEERS, SPAN + NOTE, L), BF16),
             jax.ShapeDtypeStruct((LOCAL, B, L), BF16),
         ],
-        compiler_params=params(24),
+        compiler_params=params(60),
         name="pack",
-    )(wanted, p_blocks)
+    )(wanted, p_blocks, note)
 
 
 def left_kernel(
@@ -126,10 +136,10 @@
         def place(d, at):
             here = cursor[d]
             cursor[d] = at
-            return at + ((here + GROUP - 1) // GROUP) * GROUP
+            return at + ((here + GROUP - 1) & -GROUP)
 
         total = lax.fori_loop(0, DEST, place, 0, unroll=8)
-        count_ref[0] = total // GROUP
+        count_ref[0] = total >> 2
 
         def blank(i, carry):
             code_ref[i] = 2 * NB
@@ -165,9 +175,9 @@
         cursor[d] = at + valid
         at = jnp.where(valid == 1, at, POSITIONS)
         code_ref[at] = code_in[e]
-        group_ref[at // GROUP] = d
-        tile = at // 2
-        held[tile] = jnp.where(half == at % 2, value, held[tile].astype(F32)).astype(BF16)
+        group_ref[at >> 2] = d
+        tile = at >> 1
+        held[tile] = jnp.where(half == (at & 1), value, held[tile].astype(F32)).astype(BF16)
 
     def pair_step(pair, carry):
         first = 2 * pair
@@ -176,14 +186,14 @@
         for m in range(B // 2):
             one = a_ref[first, :, pl.ds(m * L, L)].astype(F32)
             two = a_ref[second, :, pl.ds(m * L, L)].astype(F32)
-            wide[pl.ds(2 * m, ROWS_STEP, stride=B), :] = jnp.where(
+            wide[pl.ds(2 * m, ROWS_STEP, stride=PITCH), :] = jnp.where(
                 low16, one, pltpu.roll(two, B, 1)
             )
-            wide[pl.ds(2 * m + 1, ROWS_STEP, stride=B), :] = jnp.where(
+            wide[pl.ds(2 * m + 1, ROWS_STEP, stride=PITCH), :] = jnp.where(
                 low16, pltpu.roll(one, B, 1), two
             )
         for row in range(ROWS_STEP):
-            block = wide[pl.ds(row * B, B), :].astype(BF16)
+            block = wide[pl.ds(row * PITCH, B), :].astype(BF16)
             value = jnp.dot(turned_p[row], block, preferred_element_type=F32)
             turned = pltpu.roll(value, B, 1)
             insert(row, first, jnp.where(low, value, turned), 1)
@@ -217,7 +227,7 @@
             ],
             scratch_shapes=[
                 pltpu.VMEM((2 * GROUPS + 1, B, L), BF16),
-                pltpu.VMEM((ROWS_STEP * B, L), F32),
+                pltpu.VMEM((ROWS_STEP * PITCH, L), F32),
                 pltpu.VMEM((ROWS_STEP, B, B), BF16),
                 pltpu.SMEM((DEST,), jnp.int32),
                 pltpu.SemaphoreType.DMA,
@@ -247,7 +257,11 @@
     @pl.when(step == 0)
     def _():
         mine = pltpu.make_async_copy(local_hbm, blocks.at[pl.ds(0, LOCAL)], sems.at[0])
-        others = pltpu.make_async_copy(ghost_hbm, blocks.at[pl.ds(LOCAL, TILES)], sems.at[1])
+        others = pltpu.make_async_copy(
+            ghost_hbm.at[:, pl.ds(0, SPAN), :],
+            blocks.at[pl.ds(LOCAL, TILES)].reshape(PEERS, SPAN, L),
+            sems.at[1],
+        )
         mine.start()
         others.start()
         low = low_lanes((B, L))
@@ -273,14 +287,14 @@
                 parts = []
                 for w in range(GROUP):
                     code = code_ref[group * GROUP + w]
-                    parts.append(blocks[code // 2] * halves[code % 2])
+                    parts.append(blocks[code >> 1] * halves[code & 1])
                 rhs = jnp.concatenate(parts, axis=0)
                 d = group_ref[group]
                 total[d] += jnp.dot(lhs, rhs, preferred_element_type=F32)
             return carry
 
         left_over = groups - step * CHUNK
-        batches = jnp.clip((left_over + BATCH - 1) // BATCH, 0, CHUNK // BATCH)
+        batches = jnp.clip((left_over + BATCH - 1) >> 4, 0, CHUNK // BATCH)
         lax.fori_loop(0, batches, batch, 0)
 
     @pl.when(step >= STEPS)
@@ -385,28 +399,37 @@
     return dest, code
 
 
-def routes(targets, me):
-    column = targets // NCL % targets.shape[0]
+def buckets(targets, peers_y):
+    column = targets // NCL % peers_y
     order = jnp.arange(NCL)
     same = column[:, :, None] == column[:, None, :]
     earlier = order[None, None, :] < order[None, :, None]
     rank = jnp.sum((same & earlier).astype(jnp.int32), axis=2)
-    source = jnp.arange(targets.shape[0])[:, None] * CCAP + rank
-    here = (column == me)[:, :, None] & ((targets % NCL)[:, :, None] == order[None, None, :])
-    origin = jnp.sum(jnp.where(here, source[:, :, None], 0), axis=(0, 1))
-    bucket = (column * CCAP + rank)[me]
-    return bucket.astype(jnp.int32), origin.astype(jnp.int32)
+    return (column * CCAP + rank).astype(jnp.int32)
+
+
+def origins(targets, me):
+    peers_y = targets.shape[0]
+    order = jnp.arange(NCL)
+    rank = buckets(targets, peers_y) % CCAP
+    source = jnp.arange(peers_y)[:, None] * CCAP + rank
+    here = (targets // NCL % peers_y == me)[:, :, None]
+    here = here & ((targets % NCL)[:, :, None] == order[None, None, :])
+    return jnp.sum(jnp.where(here, source[:, :, None], 0), axis=(0, 1)).astype(jnp.int32)
 
 
 def body(a_blocks, p_blocks, a_source, send_list, agg_local, coarse_slot, coarse_target):
     peers_y = lax.axis_size("py")
     me = lax.axis_index("py")
-    sending, local = pack(send_list.reshape(-1), p_blocks)
-    ghost = lax.all_to_all(
-        sending.reshape(PEERS, Q // 2 * B, L), ("px", "py"), split_axis=0, concat_axis=0, tiled=True
-    ).reshape(TILES, B, L)
-    targets = lax.all_gather(coarse_target, "py")
-    bucket, origin = routes(targets, me)
+    modulus = peers_y * NCL
+    note = jnp.zeros((NOTE, L), BF16).at[0, :NCL].set((coarse_target % modulus).astype(BF16))
+    sending, local = pack(send_list.reshape(-1), p_blocks, note)
+    ghost = lax.all_to_all(sending, ("px", "py"), split_axis=0, concat_axis=0, tiled=True)
+    notes = lax.dynamic_slice(
+        ghost, (lax.axis_index("px") * peers_y, SPAN, 0), (peers_y, 1, NCL)
+    )
+    origin = origins(notes.reshape(peers_y, NCL).astype(jnp.int32), me)
+    bucket = buckets(coarse_target[None], peers_y)[0]
     dest, code = lists(a_source, agg_local, coarse_slot)
     ordered, code, group, count = left(dest, code, a_blocks.transpose(1, 0, 2), local)
     rows = right(code, group, count, bucket, ordered, local, ghost, peers_y)

time: 425 us -> 317 us (0.75)
  the two profiles are of different devices: /device:TPU:116 before, /device:TPU:124 now
where the time goes in v2:
time: 317 us; the launch traced here: 316 us
  Pallas kernels  149 us (47%)
  waiting for transfers between devices  134 us (42%)
  starting transfers between devices  25.6 us (8%)
  local copies, waits for them, and re-layouts  5.25 us (2%)
    all_to_all x1, waiting for transfers between devices, body(): lax.all_to_all(rows.reshape(peers_y, CCAP * S * B // 2, L), 'py', split_a...  119 us
    pallas_call x1, Pallas kernels, left(): pl.pallas_call(left_kernel, grid_spec=pltpu.PrefetchScalarGridSpec(num_sc...  84.2 us
    pallas_call x1, Pallas kernels, right(): pl.pallas_call(right_kernel, grid_spec=pltpu.PrefetchScalarGridSpec(num_s...  42.2 us
    all_to_all x1, starting transfers between devices, body(): lax.all_to_all(rows.reshape(peers_y, CCAP * S * B // 2, L), 'py', split_a...  15.5 us
    all_to_all x1, waiting for transfers between devices, body(): lax.all_to_all(sending, ('px', 'py'), split_axis=0, concat_axis=0, tiled=...  14.7 us
    pallas_call x1, Pallas kernels, place(): pl.pallas_call(place_kernel, grid_spec=pltpu.PrefetchScalarGridSpec(num_s...  13 us
    all_to_all x1, starting transfers between devices, body(): lax.all_to_all(sending, ('px', 'py'), split_axis=0, concat_axis=0, tiled=...  10.1 us
    pallas_call x1, Pallas kernels, pack(): pl.pallas_call(pack_kernel, grid_spec=pltpu.PrefetchScalarGridSpec(num_sc...  9.74 us
  transfers between devices with their start and end apart: 2, of which 2 were waited for; matrix products, arithmetic and copies ran while one was open for 1% of the time, Pallas kernels for 27%

profile of v2, /device:TPU:124, one launch (start us, length us, event | category | flops | bytes accessed | tf_op | source)
XLA Modules:
  0.0 316.1 jit_solution(9337949902715262696)
XLA Ops:
  0.0 0.7 and_select_fusion.2
  0.7 0.8 copy.11
  1.5 0.7 reshape.245.wanted
  2.1 0.6 scatter.4.note_ref
  2.7 9.7 %pack.1 = (bf16[128,264,128]{2,1,0:T(8,128)(2,1)}, bf16[98,64,128]{2,1,0:T(8,128)(2,1)}) custom-call(s32[1024]{0:T(1024)} %reshape.245.wanted, bf16[96,4096]{1,0:T(8,128)(2,1)} %p_ref.1, bf16[8,128]{1,0:T(8,128)(2,1)} %scatter.4.note_ref), custom_call_target="tpu_custom_call" | custom-call | tf_op jit(solution)/shard_map/pack/pallas_call | solution.py:91
  12.5 0.0 copy-start.3
  12.5 0.0 copy-start.5
  12.5 0.0 copy-start.4
  12.5 10.1 %all-to-all-start = ((bf16[128,264,128]{2,1,0:T(8,128)(2,1)}), bf16[128,264,128]{2,1,0:T(8,128)(2,1)}, u32[]{:S(2)}, u32[]{:S(2)}) async-start(bf16[128,264,128]{2,1,0:T(8,128)(2,1)} %get-tuple-element.23), calls=%async_computation | async-start | bytes 17301504 | tf_op jit(solution)/shard_map/all_to_all | solution.py:427
  22.6 0.0 copy-done.3
  22.6 0.1 copy.13
  22.7 0.8 reshape.248.code_in
  23.5 0.0 copy-done.5
  23.5 0.0 copy-done.4
  23.5 0.1 copy.12
  23.6 0.8 reshape.247.dest_in
  24.4 0.2 convert_reduce_fusion.1
  24.6 0.0 copy-start
  24.6 84.2 %left.1 = (bf16[2048,64,128]{2,1,0:T(8,128)(2,1)}, s32[4100]{0:T(1024)}, s32[1025]{0:T(1024)}, s32[1]{0:T(128)}) custom-call(s32[2592]{0:T(1024)} %reshape.247.dest_in, s32[2592]{0:T(1024)} %reshape.248.code_in, bf16[27,96,4096]{2,1,0:T(8,128)(2,1)} %bitcast.12, bf16[98,64,128]{2,1,0:T(8,128)(2,1)} %get-tuple-element.24.p_ref.local_hbm), custom_call_target="tpu_custom_call" | custom-call | flops 21743271936 | bytes 60000000 | tf_op jit(solution)/shard_map/left/pallas_call | solution.py:213
  108.8 14.7 %all-to-all-done.ghost_hbm = bf16[128,264,128]{2,1,0:T(8,128)(2,1)} async-done(((bf16[128,264,128]{2,1,0:T(8,128)(2,1)}), bf16[128,264,128]{2,1,0:T(8,128)(2,1)}, u32[]{:S(2)}, u32[]{:S(2)}) %all-to-all-start) | async-done | bytes 8650784 | tf_op jit(solution)/shard_map/all_to_all | solution.py:427
  123.4 0.0 copy-done
  123.4 0.0 copy-start.1
  123.4 0.7 copy-done.1
  124.2 0.7 copy-done.2
  124.9 42.2 %right.1 = bf16[32,27,32,128]{3,2,1,0:T(8,128)(2,1)} custom-call(s32[4100]{0:T(1024)S(1)} %copy-done.1, s32[1025]{0:T(1024)S(1)} %copy-done.2, s32[1]{0:T(128)} %get-tuple-element.27.count_ref, s32[16]{0:T(128)S(1)} %multiply_add_fusion.bucket_ref, bf16[2048,64,128]{2,1,0:T(8,128)(2,1)} %get-tuple-element.28.t_ref, bf16[98,64,128]{2,1,0:T(8,128)(2,1)S(1)} %copy-done, ...), custom_call_target="tpu_custom_call" | custom-call | tf_op jit(solution)/shard_map/right/pallas_call | solution.py:328
  167.0 15.5 %all-to-all-start.1 = ((bf16[16,1728,128]{2,1,0:T(8,128)(2,1)}), bf16[16,1728,128]{2,1,0:T(8,128)(2,1)}, u32[]{:S(2)}, u32[]{:S(2)}) async-start(bf16[16,1728,128]{2,1,0:T(8,128)(2,1)} %bitcast.8), calls=%async_computation.1 | async-start | bytes 14155776 | tf_op jit(solution)/shard_map/all_to_all | solution.py:436
  182.5 0.8 and_select_fusion
  183.4 0.4 convert_reduce_fusion
  183.8 0.1 fusion.3
  183.9 0.2 select_reduce_fusion.from_ref
  184.1 119.0 %all-to-all-done.1 = bf16[16,1728,128]{2,1,0:T(8,128)(2,1)} async-done(((bf16[16,1728,128]{2,1,0:T(8,128)(2,1)}), bf16[16,1728,128]{2,1,0:T(8,128)(2,1)}, u32[]{:S(2)}, u32[]{:S(2)}) %all-to-all-start.1) | async-done | bytes 7077920 | tf_op jit(solution)/shard_map/all_to_all | solution.py:436
  303.1 13.0 %place.1 = bf16[27,16,4096]{2,1,0:T(8,128)(2,1)} custom-call(s32[16]{0:T(128)S(1)} %select_reduce_fusion.from_ref, bf16[32,27,32,128]{3,2,1,0:T(8,128)(2,1)} %bitcast.5.in_ref), custom_call_target="tpu_custom_call" | custom-call | tf_op jit(solution)/shard_map/place/pallas_call | solution.py:376
  (8 shorter events, 0.1 us)
Async XLA Ops:
  12.5 10.1 %copy-start.3 = (s32[96,27]{0,1:T(8,128)S(1)}, s32[96,27]{0,1:T(8,128)}, u32[]{:S(2)}) copy-start(s32[96,27]{0,1:T(8,128)} %param.11) | copy-start | bytes 31108
  12.5 11.0 %copy-start.5 = (s32[96]{0:T(128)S(1)}, s32[96]{0:T(128)}, u32[]{:S(2)}) copy-start(s32[96]{0:T(128)} %param.13) | copy-start | bytes 1156
  12.5 11.0 %copy-start.4 = (s32[96,27]{0,1:T(8,128)S(1)}, s32[96,27]{0,1:T(8,128)}, u32[]{:S(2)}) copy-start(s32[96,27]{0,1:T(8,128)} %param.14) | copy-start | bytes 31108
  12.5 110.9 %all-to-all-start = ((bf16[128,264,128]{2,1,0:T(8,128)(2,1)}), bf16[128,264,128]{2,1,0:T(8,128)(2,1)}, u32[]{:S(2)}, u32[]{:S(2)}) async-start(bf16[128,264,128]{2,1,0:T(8,128)(2,1)} %get-tuple-element.23), calls=%async_computation | async-start | bytes 17301504 | tf_op jit(solution)/shard_map/all_to_all | solution.py:427
  24.6 98.9 %copy-start = (bf16[98,64,128]{2,1,0:T(8,128)(2,1)S(1)}, bf16[98,64,128]{2,1,0:T(8,128)(2,1)}, u32[]{:S(2)}) copy-start(bf16[98,64,128]{2,1,0:T(8,128)(2,1)} %get-tuple-element.24.p_ref.local_hbm) | copy-start | bytes 4816900
  123.4 0.7 copy-start.1
  124.2 0.7 copy-start.2
  167.0 136.0 %all-to-all-start.1 = ((bf16[16,1728,128]{2,1,0:T(8,128)(2,1)}), bf16[16,1728,128]{2,1,0:T(8,128)(2,1)}, u32[]{:S(2)}, u32[]{:S(2)}) async-start(bf16[16,1728,128]{2,1,0:T(8,128)(2,1)} %bitcast.8), calls=%async_computation.1 | async-start | bytes 14155776 | tf_op jit(solution)/shard_map/all_to_all | solution.py:436

commit v3 on v2

--- a/solution.py
+++ b/solution.py
@@ -1,3 +1,5 @@
+import functools
+
 import jax
 import jax.numpy as jnp
 from jax import lax
@@ -16,6 +18,8 @@
 NCL = NB // AGG
 PEERS = 128
 DEST = NCL * S
+PARTS = ((0, 9), (9, 18))
+SIDE = 4
 GROUP = 4
 TILES = PEERS * Q // 2
 LOCAL = NB + 2
@@ -26,6 +30,8 @@
 SPAN = Q // 2 * B
 NOTE = 8
 BATCH = 16
+CHUNK_BITS = 7
+BATCH_BITS = 4
 STEPS = GROUPS // CHUNK
 ROWS_STEP = 16
 F32 = jnp.float32
@@ -138,8 +144,12 @@
             cursor[d] = at
             return at + ((here + GROUP - 1) & -GROUP)
 
-        total = lax.fori_loop(0, DEST, place, 0, unroll=8)
-        count_ref[0] = total >> 2
+        at = 0
+        for n, (start, width) in enumerate(PARTS):
+            count_ref[2 * n] = at >> 2
+            at = lax.fori_loop(start * NCL, (start + width) * NCL, place, at, unroll=8)
+            count_ref[2 * n + 1] = at >> 2
+            at = (at + GROUP * BATCH - 1) & -(GROUP * BATCH)
 
         def blank(i, carry):
             code_ref[i] = 2 * NB
@@ -237,7 +247,7 @@
             jax.ShapeDtypeStruct((2 * GROUPS, B, L), BF16),
             jax.ShapeDtypeStruct((POSITIONS + GROUP,), jnp.int32),
             jax.ShapeDtypeStruct((GROUPS + 1,), jnp.int32),
-            jax.ShapeDtypeStruct((1,), jnp.int32),
+            jax.ShapeDtypeStruct((2 * len(PARTS),), jnp.int32),
         ],
         compiler_params=params(56),
         cost_estimate=pl.CostEstimate(
@@ -248,11 +258,14 @@
 
 
 def right_kernel(
-    code_ref, group_ref, count_ref, bucket_ref, t_ref, local_hbm, ghost_hbm, out_ref,
-    blocks, total, wide, halves, sems,
+    part, code_ref, group_ref, count_ref, bucket_ref, t_ref, local_hbm, ghost_hbm, out_hbm,
+    blocks, total, wide, staged, halves, sems, out_sems,
 ):
     step = pl.program_id(0)
-    groups = count_ref[0]
+    start, width = PARTS[part]
+    first = count_ref[2 * part]
+    last = count_ref[2 * part + 1]
+    origin = (first >> CHUNK_BITS) << CHUNK_BITS
 
     @pl.when(step == 0)
     def _():
@@ -264,7 +277,7 @@
         )
         mine.start()
         others.start()
-        low = low_lanes((B, L))
+        low = low_lanes((16, L))
         halves[0] = jnp.where(low, 1.0, 0.0).astype(BF16)
         halves[1] = jnp.where(low, 0.0, 1.0).astype(BF16)
         zero = jnp.zeros((B, L), F32)
@@ -273,96 +286,174 @@
             total[i] = zero
             return carry
 
-        lax.fori_loop(0, DEST + 1, clear, 0, unroll=8)
+        lax.fori_loop(0, width * NCL + 1, clear, 0, unroll=8)
         mine.wait()
         others.wait()
 
-    @pl.when(step < STEPS)
-    def _():
-        def batch(b, carry):
-            for u in range(BATCH):
-                here = b * BATCH + u
-                group = step * CHUNK + here
-                lhs = jnp.concatenate([t_ref[2 * here], t_ref[2 * here + 1]], axis=1)
-                parts = []
-                for w in range(GROUP):
-                    code = code_ref[group * GROUP + w]
-                    parts.append(blocks[code >> 1] * halves[code & 1])
-                rhs = jnp.concatenate(parts, axis=0)
-                d = group_ref[group]
-                total[d] += jnp.dot(lhs, rhs, preferred_element_type=F32)
-            return carry
-
-        left_over = groups - step * CHUNK
-        batches = jnp.clip((left_over + BATCH - 1) >> 4, 0, CHUNK // BATCH)
-        lax.fori_loop(0, batches, batch, 0)
-
-    @pl.when(step >= STEPS)
-    def _():
-        base = (step - STEPS) * S
+    def batch(b, carry):
+        for u in range(BATCH):
+            here = b * BATCH + u
+            group = origin + step * CHUNK + here
+            lhs = jnp.concatenate([t_ref[2 * here], t_ref[2 * here + 1]], axis=1)
+            parts = []
+            for w in range(GROUP):
+                code = code_ref[group * GROUP + w]
+                block = blocks[code >> 1].reshape(B // 16, 16, L)
+                parts.append((block * halves[code & 1][None]).reshape(B, L))
+            rhs = jnp.concatenate(parts, axis=0)
+            d = jnp.minimum(group_ref[group] - start * NCL, width * NCL)
+            total[d] += jnp.dot(lhs, rhs, preferred_element_type=F32)
+        return carry
+
+    at = origin + step * CHUNK
+    begin = jnp.clip((first - at) >> BATCH_BITS, 0, CHUNK // BATCH)
+    end = jnp.clip((last - at + BATCH - 1) >> BATCH_BITS, 0, CHUNK // BATCH)
+    lax.fori_loop(begin, end, batch, 0)
+
+    @pl.when(step == STEPS - 1)
+    def _():
         low = low_lanes((B // 2, L))
-
-        def emit(part, carry):
-            for u in range(9):
-                s = part * 9 + u
-                value = total[base + s]
-                wide[pl.ds(u * B, B), :] = value + pltpu.roll(value, B, 1)
-                even = wide[pl.ds(u * B, B // 2, stride=2), :]
-                odd = wide[pl.ds(u * B + 1, B // 2, stride=2), :]
-                out_ref[0, s] = jnp.where(low, even, odd).astype(BF16)
-            return carry
-
-        lax.fori_loop(0, S // 9, emit, 0)
-
-
-def right(code, group, count, bucket, ordered, local, ghost, peers_y):
-    last = STEPS - 1
+        copies = [
+            pltpu.make_async_copy(staged.at[c], out_hbm.at[bucket_ref[c]], out_sems.at[c])
+            for c in range(NCL)
+        ]
+        for c in range(NCL):
+
+            def emit(s, carry, c=c):
+                value = total[s * NCL + c]
+                row = pl.multiple_of(s * B, B)
+                wide[pl.ds(row, B), :] = value + pltpu.roll(value, B, 1)
+                even = wide[pl.ds(row, B // 2, stride=2), :]
+                odd = wide[pl.ds(row + 1, B // 2, stride=2), :]
+                staged[c, s] = jnp.where(low, even, odd).astype(BF16)
+                return carry
+
+            lax.fori_loop(0, width, emit, 0, unroll=True)
+            copies[c].start()
+        for copy in copies:
+            copy.wait()
+
+
+def right(part, code, group, count, bucket, ordered, local, ghost, peers_y):
+    width = PARTS[part][1]
 
     def t_map(i, code_ref, group_ref, count_ref, bucket_ref):
-        used = jnp.maximum((count_ref[0] + CHUNK - 1) // CHUNK - 1, 0)
-        return (jnp.minimum(jnp.minimum(i, last), used), 0, 0)
-
-    def out_map(i, code_ref, group_ref, count_ref, bucket_ref):
-        return (bucket_ref[jnp.maximum(i - STEPS, 0)], 0, 0, 0)
+        block = (count_ref[2 * part] >> CHUNK_BITS) + i
+        used = jnp.maximum(count_ref[2 * part + 1] - 1, 0) >> CHUNK_BITS
+        return (jnp.minimum(block, used), 0, 0)
 
     return pl.pallas_call(
-        right_kernel,
+        functools.partial(right_kernel, part),
         grid_spec=pltpu.PrefetchScalarGridSpec(
             num_scalar_prefetch=4,
-            grid=(STEPS + NCL,),
+            grid=(STEPS,),
             in_specs=[
                 pl.BlockSpec((2 * CHUNK, B, L), t_map),
                 pl.BlockSpec(memory_space=pl.ANY),
                 pl.BlockSpec(memory_space=pl.ANY),
             ],
-            out_specs=pl.BlockSpec((1, S, B // 2, L), out_map),
+            out_specs=pl.BlockSpec(memory_space=pl.ANY),
             scratch_shapes=[
                 pltpu.VMEM((LOCAL + TILES, B, L), BF16),
-                pltpu.VMEM((DEST + 1, B, L), F32),
-                pltpu.VMEM((9 * B, L), F32),
-                pltpu.VMEM((2, B, L), BF16),
+                pltpu.VMEM((width * NCL + 1, B, L), F32),
+                pltpu.VMEM((width * B, L), F32),
+                pltpu.VMEM((NCL, width, B // 2, L), BF16),
+                pltpu.VMEM((2, 16, L), BF16),
                 pltpu.SemaphoreType.DMA((2,)),
-            ],
-        ),
-        out_shape=jax.ShapeDtypeStruct((peers_y * CCAP, S, B // 2, L), BF16),
-        compiler_params=params(48),
-        name="right",
+                pltpu.SemaphoreType.DMA((NCL,)),
+            ],
+        ),
+        out_shape=jax.ShapeDtypeStruct((peers_y * CCAP, width, B // 2, L), BF16),
+        compiler_params=params(60),
+        cost_estimate=pl.CostEstimate(
+            flops=NB * K * B**3 * 32, bytes_accessed=30_000_000, transcendentals=0
+        ),
+        name="right%d" % part,
     )(code, group, count, bucket, ordered, local, ghost)
 
 
-def place_kernel(from_ref, in_ref, out_ref, wide):
+def exchange_kernel(x_ref, out_ref, send_sems, recv_sems, own_sem):
+    px, me = lax.axis_index("px"), lax.axis_index("py")
+    shifts = sorted(
+        ((dx, dy) for dx in range(SIDE) for dy in range(SIDE) if dx or dy),
+        key=lambda o: -min(o[0], SIDE - o[0]) - min(o[1], SIDE - o[1]),
+    )
+
+    def peer(shift):
+        return (me // SIDE + shift[0]) % SIDE * SIDE + (me + shift[1]) % SIDE
+
+    barrier = pltpu.get_barrier_semaphore()
+    for shift in shifts:
+        pl.semaphore_signal(
+            barrier, inc=1, device_id=(px, peer(shift)), device_id_type=pl.DeviceIdType.MESH
+        )
+    pl.semaphore_wait(barrier, len(shifts))
+    copies = []
+    for n, shift in enumerate(shifts):
+        copy = pltpu.make_async_remote_copy(
+            src_ref=x_ref.at[peer(shift)],
+            dst_ref=out_ref.at[me],
+            send_sem=send_sems.at[n],
+            recv_sem=recv_sems.at[n],
+            device_id=(px, peer(shift)),
+            device_id_type=pl.DeviceIdType.MESH,
+        )
+        copy.start()
+        copies.append(copy)
+    own = pltpu.make_async_copy(x_ref.at[me], out_ref.at[me], own_sem)
+    own.start()
+    own.wait()
+    for copy in copies:
+        copy.wait()
+
+
+def exchange(rows):
+    peers = SIDE * SIDE
+    return pl.pallas_call(
+        exchange_kernel,
+        in_specs=[pl.BlockSpec(memory_space=pl.ANY)],
+        out_specs=pl.BlockSpec(memory_space=pl.ANY),
+        out_shape=jax.ShapeDtypeStruct(rows.shape, rows.dtype),
+        scratch_shapes=[
+            pltpu.SemaphoreType.DMA((peers - 1,)),
+            pltpu.SemaphoreType.DMA((peers - 1,)),
+            pltpu.SemaphoreType.DMA,
+        ],
+        compiler_params=pltpu.CompilerParams(
+            collective_id=0, has_side_effects=True, vmem_limit_bytes=60 * 1024 * 1024
+        ),
+        cost_estimate=pl.CostEstimate(
+            flops=0, bytes_accessed=300_000_000, transcendentals=0
+        ),
+        name="exchange",
+    )(rows)
+
+
+AHEAD = 4
+
+
+def place_kernel(from_ref, *refs):
+    ins, out_ref, wide = refs[:-2], refs[-2], refs[-1]
     step = pl.program_id(0)
     span = NCL * B // 2
 
-    @pl.when(step < NCL)
-    def _():
-        for s in range(S):
-            wide[pl.ds(s * span + step, B // 2, stride=NCL), :] = in_ref[0, s].astype(F32)
-
-    @pl.when(step >= NCL)
+    @pl.when(step < NCL // AHEAD)
+    def _():
+        for n, (start, width) in enumerate(PARTS):
+            for j in range(AHEAD):
+                rows = ins[n * AHEAD + j]
+
+                def spread(s, carry, start=start, rows=rows, j=j):
+                    at = (start + s) * span + step * AHEAD + j
+                    wide[pl.ds(at, B // 2, stride=NCL), :] = rows[0, s].astype(F32)
+                    return carry
+
+                lax.fori_loop(0, width, spread, 0, unroll=True)
+
+    @pl.when(step >= NCL // AHEAD)
     def _():
         def flatten(u, carry):
-            start = pl.multiple_of(((step - NCL) * 9 + u) * span, span)
+            start = pl.multiple_of(((step - NCL // AHEAD) * 9 + u) * span, span)
             for m in range(B // 2):
                 out_ref[u, :, pl.ds(m * L, L)] = wide[
                     pl.ds(start + m * NCL, NCL), :
@@ -373,27 +464,33 @@
 
 
 def place(origin, arrived):
+    turns = NCL // AHEAD
+
+    def spec(width, j):
+        return pl.BlockSpec(
+            (1, width, B // 2, L),
+            lambda i, o: (o[jnp.minimum(i, turns - 1) * AHEAD + j], 0, 0, 0),
+        )
+
     return pl.pallas_call(
         place_kernel,
         grid_spec=pltpu.PrefetchScalarGridSpec(
             num_scalar_prefetch=1,
-            grid=(NCL + S // 9,),
-            in_specs=[
-                pl.BlockSpec(
-                    (1, S, B // 2, L), lambda i, o: (o[jnp.minimum(i, NCL - 1)], 0, 0, 0)
-                )
-            ],
-            out_specs=pl.BlockSpec((9, NCL, B * B), lambda i, o: (jnp.maximum(i - NCL, 0), 0, 0)),
+            grid=(turns + S // 9,),
+            in_specs=[spec(width, j) for _, width in PARTS for j in range(AHEAD)],
+            out_specs=pl.BlockSpec(
+                (9, NCL, B * B), lambda i, o: (jnp.maximum(i - turns, 0), 0, 0)
+            ),
             scratch_shapes=[pltpu.VMEM((S * NCL * B // 2, L), F32)],
         ),
         out_shape=jax.ShapeDtypeStruct((S, NCL, B * B), BF16),
-        compiler_params=params(32),
+        compiler_params=params(60),
         name="place",
-    )(origin, arrived)
+    )(origin, *[rows for rows in arrived for _ in range(AHEAD)])
 
 
 def lists(a_source, agg_local, coarse_slot):
-    dest = (agg_local[:, None] * S + coarse_slot).reshape(-1)
+    dest = (coarse_slot * NCL + agg_local[:, None]).reshape(-1)
     ghost = a_source - NB + 2 * LOCAL
     code = jnp.where(a_source < NB, 2 * a_source, ghost).reshape(-1)
     return dest, code
@@ -432,10 +529,15 @@
     bucket = buckets(coarse_target[None], peers_y)[0]
     dest, code = lists(a_source, agg_local, coarse_slot)
     ordered, code, group, count = left(dest, code, a_blocks.transpose(1, 0, 2), local)
-    rows = right(code, group, count, bucket, ordered, local, ghost, peers_y)
-    arrived = lax.all_to_all(
-        rows.reshape(peers_y, CCAP * S * B // 2, L), "py", split_axis=0, concat_axis=0, tiled=True
-    ).reshape(peers_y * CCAP, S, B // 2, L)
+    arrived = []
+    for part, (_, width) in enumerate(PARTS):
+        rows = right(part, code, group, count, bucket, ordered, local, ghost, peers_y)
+        rows = rows.reshape(peers_y, CCAP * width * B // 2, L)
+        if part == 0:
+            rows = lax.all_to_all(rows, "py", split_axis=0, concat_axis=0, tiled=True)
+        else:
+            rows = exchange(rows)
+        arrived.append(rows.reshape(peers_y * CCAP, width, B // 2, L))
     return place(origin, arrived).transpose(1, 0, 2)
 
 

time: 317 us -> 269 us (0.85)
  the two profiles are of different devices: /device:TPU:124 before, /device:TPU:2 now
where the time goes in v3:
time: 269 us; the launch traced here: 266 us
  Pallas kernels  217 us (81%)
  starting transfers between devices  23.4 us (9%)
  waiting for transfers between devices  17.1 us (6%)
  local copies, waits for them, and re-layouts  5.24 us (2%)
  other arithmetic  3.59 us (1%)
    pallas_call x1, Pallas kernels, left(): pl.pallas_call(left_kernel, grid_spec=pltpu.PrefetchScalarGridSpec(num_sc...  84.1 us
    pallas_call x1, Pallas kernels, exchange(): pl.pallas_call(exchange_kernel, in_specs=[pl.BlockSpec(memory_space=pl.AN...  69.7 us
    pallas_call x2, Pallas kernels, right(): pl.pallas_call(functools.partial(right_kernel, part), grid_spec=pltpu.Pre...  44.2 us
    all_to_all x1, waiting for transfers between devices, body(): lax.all_to_all(sending, ('px', 'py'), split_axis=0, concat_axis=0, tiled=...  17.1 us
    all_to_all x1, starting transfers between devices, body(): rows = lax.all_to_all(rows, 'py', split_axis=0, concat_axis=0, tiled=True)  12.5 us
    all_to_all x1, starting transfers between devices, body(): lax.all_to_all(sending, ('px', 'py'), split_axis=0, concat_axis=0, tiled=...  10.9 us
    pallas_call x1, Pallas kernels, pack(): pl.pallas_call(pack_kernel, grid_spec=pltpu.PrefetchScalarGridSpec(num_sc...  9.77 us
    pallas_call x1, Pallas kernels, place(): pl.pallas_call(place_kernel, grid_spec=pltpu.PrefetchScalarGridSpec(num_s...  8.82 us
  transfers between devices with their start and end apart: 2, of which 1 were waited for; matrix products, arithmetic and copies ran while one was open for 2% of the time, Pallas kernels for 68%

profile of v3, /device:TPU:2, one launch (start us, length us, event | category | flops | bytes accessed | tf_op | source)
XLA Modules:
  0.0 266.1 jit_solution(7644183980112950529)
XLA Ops:
  0.0 0.7 and_select_fusion.2
  0.7 0.8 copy.11
  1.5 0.7 reshape.250.wanted
  2.1 0.6 scatter.4.note_ref
  2.7 9.8 %pack.1 = (bf16[128,264,128]{2,1,0:T(8,128)(2,1)}, bf16[98,64,128]{2,1,0:T(8,128)(2,1)}) custom-call(s32[1024]{0:T(1024)} %reshape.250.wanted, bf16[96,4096]{1,0:T(8,128)(2,1)} %p_ref.1, bf16[8,128]{1,0:T(8,128)(2,1)} %scatter.4.note_ref), custom_call_target="tpu_custom_call" | custom-call | tf_op jit(solution)/shard_map/pack/pallas_call | solution.py:97
  12.5 0.0 copy-start.1
  12.5 0.0 copy-start.3
  12.5 0.0 copy-start.2
  12.5 10.9 %all-to-all-start = ((bf16[128,264,128]{2,1,0:T(8,128)(2,1)}), bf16[128,264,128]{2,1,0:T(8,128)(2,1)}, u32[]{:S(2)}, u32[]{:S(2)}) async-start(bf16[128,264,128]{2,1,0:T(8,128)(2,1)} %get-tuple-element.23), calls=%async_computation | async-start | bytes 17301504 | tf_op jit(solution)/shard_map/all_to_all | solution.py:524
  23.5 0.0 copy-done.1
  23.5 0.0 copy-done.3
  23.5 0.1 copy.12
  23.6 0.8 reshape.252.dest_in
  24.4 0.0 copy-done.2
  24.4 0.1 copy.13
  24.5 0.8 reshape.253.code_in
  25.2 0.2 convert_reduce_fusion.1
  25.4 0.6 multiply_add_fusion.1.bucket_ref
  26.0 84.1 %left.1 = (bf16[2048,64,128]{2,1,0:T(8,128)(2,1)}, s32[4100]{0:T(1024)}, s32[1025]{0:T(1024)}, s32[4]{0:T(128)}) custom-call(s32[2592]{0:T(1024)} %reshape.252.dest_in, s32[2592]{0:T(1024)} %reshape.253.code_in, bf16[27,96,4096]{2,1,0:T(8,128)(2,1)} %bitcast.23, bf16[98,64,128]{2,1,0:T(8,128)(2,1)} %get-tuple-element.24.p_ref.local_hbm), custom_call_target="tpu_custom_call" | custom-call | flops 21743271936 | bytes 60000000 | tf_op jit(solution)/shard_map/left/pallas_call | solution.py:223
  110.1 17.1 %all-to-all-done.ghost_hbm = bf16[128,264,128]{2,1,0:T(8,128)(2,1)} async-done(((bf16[128,264,128]{2,1,0:T(8,128)(2,1)}), bf16[128,264,128]{2,1,0:T(8,128)(2,1)}, u32[]{:S(2)}, u32[]{:S(2)}) %all-to-all-start) | async-done | bytes 8650784 | tf_op jit(solution)/shard_map/all_to_all | solution.py:524
  127.2 17.4 %right0.1 = bf16[32,9,32,128]{3,2,1,0:T(8,128)(2,1)} custom-call(s32[4100]{0:T(1024)} %get-tuple-element.25.code_ref, s32[1025]{0:T(1024)} %get-tuple-element.26.group_ref, s32[4]{0:T(128)} %get-tuple-element.27.count_ref, s32[16]{0:T(128)} %multiply_add_fusion.1.bucket_ref, bf16[2048,64,128]{2,1,0:T(8,128)(2,1)} %get-tuple-element.28.t_ref, ...), custom_call_target="tpu_custom_call" | custom-call | flops 21743271936 | bytes 30000000 | tf_op jit(solution)/shard_map/right0/pallas_call | solution.py:345
  144.6 12.5 %all-to-all-start.1 = ((bf16[16,576,128]{2,1,0:T(8,128)(2,1)}), bf16[16,576,128]{2,1,0:T(8,128)(2,1)S(1)}, u32[]{:S(2)}, u32[]{:S(2)}) async-start(bf16[16,576,128]{2,1,0:T(8,128)(2,1)} %bitcast.19), calls=%async_computation.1 | async-start | bytes 4718592 | tf_op jit(solution)/shard_map/all_to_all | solution.py:537
  157.1 26.9 %right1.1 = bf16[32,18,32,128]{3,2,1,0:T(8,128)(2,1)} custom-call(s32[4100]{0:T(1024)} %get-tuple-element.25.code_ref, s32[1025]{0:T(1024)} %get-tuple-element.26.group_ref, s32[4]{0:T(128)} %get-tuple-element.27.count_ref, s32[16]{0:T(128)} %multiply_add_fusion.1.bucket_ref, bf16[2048,64,128]{2,1,0:T(8,128)(2,1)} %get-tuple-element.28.t_ref, ...), custom_call_target="tpu_custom_call" | custom-call | flops 21743271936 | bytes 30000000 | tf_op jit(solution)/shard_map/right1/pallas_call | solution.py:345
  183.9 69.7 %exchange.1 = bf16[16,1152,128]{2,1,0:T(8,128)(2,1)} custom-call(bf16[16,1152,128]{2,1,0:T(8,128)(2,1)} %bitcast.18), custom_call_target="tpu_custom_call" | custom-call | bytes 300000000 | tf_op jit(solution)/shard_map/exchange/pallas_call | solution.py:412
  253.6 0.8 and_select_fusion
  254.5 0.4 convert_reduce_fusion
  255.0 0.1 fusion.3
  255.0 0.8 select_reduce_fusion.from_ref
  255.8 0.0 all-to-all-done.1
  255.8 0.0 copy-start
  255.8 1.4 copy-done
  257.2 8.8 %place.1 = bf16[27,16,4096]{2,1,0:T(8,128)(2,1)} custom-call(s32[16]{0:T(128)} %select_reduce_fusion.from_ref, bf16[32,9,32,128]{3,2,1,0:T(8,128)(2,1)} %bitcast.14, bf16[32,9,32,128]{3,2,1,0:T(8,128)(2,1)} %bitcast.15, bf16[32,9,32,128]{3,2,1,0:T(8,128)(2,1)} %bitcast.16, bf16[32,9,32,128]{3,2,1,0:T(8,128)(2,1)} %bitcast.17, ...), custom_call_target="tpu_custom_call" | custom-call | tf_op jit(solution)/shard_map/place/pallas_call | solution.py:475
  (5 shorter events, 0.0 us)
Async XLA Ops:
  12.5 11.0 %copy-start.1 = (s32[96,27]{0,1:T(8,128)S(1)}, s32[96,27]{0,1:T(8,128)}, u32[]{:S(2)}) copy-start(s32[96,27]{0,1:T(8,128)} %param.14) | copy-start | bytes 31108
  12.5 11.0 %copy-start.3 = (s32[96]{0:T(128)S(1)}, s32[96]{0:T(128)}, u32[]{:S(2)}) copy-start(s32[96]{0:T(128)} %param.13) | copy-start | bytes 1156
  12.5 11.9 %copy-start.2 = (s32[96,27]{0,1:T(8,128)S(1)}, s32[96,27]{0,1:T(8,128)}, u32[]{:S(2)}) copy-start(s32[96,27]{0,1:T(8,128)} %param.11) | copy-start | bytes 31108
  12.5 114.7 %all-to-all-start = ((bf16[128,264,128]{2,1,0:T(8,128)(2,1)}), bf16[128,264,128]{2,1,0:T(8,128)(2,1)}, u32[]{:S(2)}, u32[]{:S(2)}) async-start(bf16[128,264,128]{2,1,0:T(8,128)(2,1)} %get-tuple-element.23), calls=%async_computation | async-start | bytes 17301504 | tf_op jit(solution)/shard_map/all_to_all | solution.py:524
  144.6 111.2 %all-to-all-start.1 = ((bf16[16,576,128]{2,1,0:T(8,128)(2,1)}), bf16[16,576,128]{2,1,0:T(8,128)(2,1)S(1)}, u32[]{:S(2)}, u32[]{:S(2)}) async-start(bf16[16,576,128]{2,1,0:T(8,128)(2,1)} %bitcast.19), calls=%async_computation.1 | async-start | bytes 4718592 | tf_op jit(solution)/shard_map/all_to_all | solution.py:537
  255.8 1.4 copy-start

commit v4 on v3

--- a/solution.py
+++ b/solution.py
@@ -48,7 +48,7 @@
     )
 
 
-def pack_kernel(wanted, p_ref, note_ref, send_ref, local_ref, wide):
+def pack_kernel(wanted, p_ref, send_ref, local_ref, wide):
     step = pl.program_id(0)
 
     @pl.when(step == 0)
@@ -78,21 +78,19 @@
 
     def fill(peer, carry):
         for u in range(Q // 2):
-            slot = (step * per_step + peer) * Q + 2 * u
-            first = wanted[slot]
-            second = wanted[slot + 1]
+            first = wanted[2 * u, step * per_step + peer]
+            second = wanted[2 * u + 1, step * per_step + peer]
             first = jnp.where(first < 0, NB, first)
             second = jnp.where(second < 0, NB, second)
             send_ref[peer, u * B : (u + 1) * B] = jnp.where(
                 low, local_ref[first], local_ref[second]
             )
-        send_ref[peer, SPAN:] = note_ref[...]
         return carry
 
     lax.fori_loop(0, per_step, fill, 0, unroll=2)
 
 
-def pack(wanted, p_blocks, note):
+def pack(wanted, p_blocks):
     per_step = PEERS // 8
     return pl.pallas_call(
         pack_kernel,
@@ -101,21 +99,20 @@
             grid=(PEERS // per_step,),
             in_specs=[
                 pl.BlockSpec((NB, B * B), lambda i, w: (0, 0)),
-                pl.BlockSpec((NOTE, L), lambda i, w: (0, 0)),
             ],
             out_specs=[
-                pl.BlockSpec((per_step, SPAN + NOTE, L), lambda i, w: (i, 0, 0)),
+                pl.BlockSpec((per_step, SPAN, L), lambda i, w: (i, 0, 0)),
                 pl.BlockSpec((LOCAL, B, L), lambda i, w: (0, 0, 0)),
             ],
             scratch_shapes=[pltpu.VMEM((ROWS_STEP * PITCH, L), F32)],
         ),
         out_shape=[
-            jax.ShapeDtypeStruct((PEERS, SPAN + NOTE, L), BF16),
+            jax.ShapeDtypeStruct((PEERS, SPAN, L), BF16),
             jax.ShapeDtypeStruct((LOCAL, B, L), BF16),
         ],
         compiler_params=params(60),
         name="pack",
-    )(wanted, p_blocks, note)
+    )(wanted, p_blocks)
 
 
 def left_kernel(
@@ -271,7 +268,7 @@
     def _():
         mine = pltpu.make_async_copy(local_hbm, blocks.at[pl.ds(0, LOCAL)], sems.at[0])
         others = pltpu.make_async_copy(
-            ghost_hbm.at[:, pl.ds(0, SPAN), :],
+            ghost_hbm,
             blocks.at[pl.ds(LOCAL, TILES)].reshape(PEERS, SPAN, L),
             sems.at[1],
         )
@@ -364,7 +361,7 @@
             ],
         ),
         out_shape=jax.ShapeDtypeStruct((peers_y * CCAP, width, B // 2, L), BF16),
-        compiler_params=params(60),
+        compiler_params=params(63),
         cost_estimate=pl.CostEstimate(
             flops=NB * K * B**3 * 32, bytes_accessed=30_000_000, transcendentals=0
         ),
@@ -407,7 +404,7 @@
         copy.wait()
 
 
-def exchange(rows):
+def exchange(rows, collective_id, name):
     peers = SIDE * SIDE
     return pl.pallas_call(
         exchange_kernel,
@@ -420,12 +417,12 @@
             pltpu.SemaphoreType.DMA,
         ],
         compiler_params=pltpu.CompilerParams(
-            collective_id=0, has_side_effects=True, vmem_limit_bytes=60 * 1024 * 1024
+            collective_id=collective_id, has_side_effects=True, vmem_limit_bytes=63 * 1024 * 1024
         ),
         cost_estimate=pl.CostEstimate(
             flops=0, bytes_accessed=300_000_000, transcendentals=0
         ),
-        name="exchange",
+        name=name,
     )(rows)
 
 
@@ -518,17 +515,16 @@
 def body(a_blocks, p_blocks, a_source, send_list, agg_local, coarse_slot, coarse_target):
     peers_y = lax.axis_size("py")
     me = lax.axis_index("py")
-    modulus = peers_y * NCL
-    note = jnp.zeros((NOTE, L), BF16).at[0, :NCL].set((coarse_target % modulus).astype(BF16))
-    sending, local = pack(send_list.reshape(-1), p_blocks, note)
+    sending, local = pack(send_list.reshape(PEERS, Q).T, p_blocks)
     ghost = lax.all_to_all(sending, ("px", "py"), split_axis=0, concat_axis=0, tiled=True)
-    notes = lax.dynamic_slice(
-        ghost, (lax.axis_index("px") * peers_y, SPAN, 0), (peers_y, 1, NCL)
-    )
-    origin = origins(notes.reshape(peers_y, NCL).astype(jnp.int32), me)
     bucket = buckets(coarse_target[None], peers_y)[0]
     dest, code = lists(a_source, agg_local, coarse_slot)
     ordered, code, group, count = left(dest, code, a_blocks.transpose(1, 0, 2), local)
+    tied, _ = lax.optimization_barrier((coarse_target, count))
+    note = jnp.broadcast_to(jnp.pad(tied, (0, L - NCL)), (peers_y, NOTE, L))
+    targets = exchange(note, 1, "targets")[:, 0, :NCL]
+    origin = origins(targets, me)
+    bucket = jnp.concatenate([bucket, origin])
     arrived = []
     for part, (_, width) in enumerate(PARTS):
         rows = right(part, code, group, count, bucket, ordered, local, ghost, peers_y)
@@ -536,7 +532,7 @@
         if part == 0:
             rows = lax.all_to_all(rows, "py", split_axis=0, concat_axis=0, tiled=True)
         else:
-            rows = exchange(rows)
+            rows = exchange(rows, 0, "exchange")
         arrived.append(rows.reshape(peers_y * CCAP, width, B // 2, L))
     return place(origin, arrived).transpose(1, 0, 2)
 

time: 269 us -> 256 us (0.952)
  waiting for transfers between devices: 17.1 us -> 0.01 us
  Pallas kernels: 217 us -> 228 us
  starting transfers between devices: 23.4 us -> 18.7 us
  local copies, waits for them, and re-layouts: 5.24 us -> 2.38 us
    all_to_all x1, waiting for transfers between devices: 17.1 us -> 0.01 us  [body(): lax.all_to_all(sending, ('px', 'py'), split_axis=0, concat_axis=0, tiled=...]
    pallas_call x1 -> x2, Pallas kernels: 69.7 us -> 81.4 us  [exchange(): pl.pallas_call(exchange_kernel, in_specs=[pl.BlockSpec(memory_space=pl.AN...]
    all_to_all x1, starting transfers between devices: 12.5 us -> 7.67 us  [body(): rows = lax.all_to_all(rows, 'py', split_axis=0, concat_axis=0, tiled=True)]
  transfers between devices with their start and end apart: 2 -> 2, of which waited for: 1 -> 0; matrix products, arithmetic and copies ran while one was open for 2% -> 2% of each run, Pallas kernels for 68% -> 76%
where the time goes in v4:
time: 256 us; the launch traced here: 252 us
  Pallas kernels  228 us (89%)
  starting transfers between devices  18.7 us (7%)
    pallas_call x1, Pallas kernels, left(): pl.pallas_call(left_kernel, grid_spec=pltpu.PrefetchScalarGridSpec(num_sc...  84.2 us
    pallas_call x2, Pallas kernels, exchange(): pl.pallas_call(exchange_kernel, in_specs=[pl.BlockSpec(memory_space=pl.AN...  81.4 us
    pallas_call x2, Pallas kernels, right(): pl.pallas_call(functools.partial(right_kernel, part), grid_spec=pltpu.Pre...  44.3 us
    all_to_all x1, starting transfers between devices, body(): lax.all_to_all(sending, ('px', 'py'), split_axis=0, concat_axis=0, tiled=...  11 us
    pallas_call x1, Pallas kernels, pack(): pl.pallas_call(pack_kernel, grid_spec=pltpu.PrefetchScalarGridSpec(num_sc...  9.76 us
    pallas_call x1, Pallas kernels, place(): pl.pallas_call(place_kernel, grid_spec=pltpu.PrefetchScalarGridSpec(num_s...  8.82 us
    all_to_all x1, starting transfers between devices, body(): rows = lax.all_to_all(rows, 'py', split_axis=0, concat_axis=0, tiled=True)  7.67 us
  transfers between devices with their start and end apart: 2, of which 0 were waited for; matrix products, arithmetic and copies ran while one was open for 2% of the time, Pallas kernels for 76%

profile of v4, /device:TPU:2, one launch (start us, length us, event | category | flops | bytes accessed | tf_op | source)
XLA Modules:
  0.0 252.2 jit_solution(11040282603158633433)
XLA Ops:
  0.0 9.8 %pack.1 = (bf16[128,256,128]{2,1,0:T(8,128)(2,1)}, bf16[98,64,128]{2,1,0:T(8,128)(2,1)}) custom-call(s32[8,128]{1,0:T(8,128)} %bitcast.20, bf16[96,4096]{1,0:T(8,128)(2,1)} %p_ref.1), custom_call_target="tpu_custom_call" | custom-call | tf_op jit(solution)/shard_map/pack/pallas_call | solution.py:95
  9.8 0.0 copy-start
  9.8 0.0 copy-start.3
  9.8 0.0 copy-start.1
  9.8 11.0 %all-to-all-start = ((bf16[128,256,128]{2,1,0:T(8,128)(2,1)}), bf16[128,256,128]{2,1,0:T(8,128)(2,1)}, u32[]{:S(2)}, u32[]{:S(2)}) async-start(bf16[128,256,128]{2,1,0:T(8,128)(2,1)} %get-tuple-element.18), calls=%async_computation | async-start | bytes 16777216 | tf_op jit(solution)/shard_map/all_to_all | solution.py:519
  20.8 0.0 copy-done
  20.8 0.0 copy-done.3
  20.8 0.1 copy.10
  20.9 0.8 reshape.244.dest_in
  21.7 0.0 copy-done.1
  21.7 0.1 copy.11
  21.8 0.8 reshape.245.code_in
  22.5 0.0 copy-start.4
  22.6 84.2 %left.1 = (bf16[2048,64,128]{2,1,0:T(8,128)(2,1)}, s32[4100]{0:T(1024)}, s32[1025]{0:T(1024)}, s32[4]{0:T(128)}) custom-call(s32[2592]{0:T(1024)} %reshape.244.dest_in, s32[2592]{0:T(1024)} %reshape.245.code_in, bf16[27,96,4096]{2,1,0:T(8,128)(2,1)} %bitcast.21, bf16[98,64,128]{2,1,0:T(8,128)(2,1)} %get-tuple-element.12.p_ref.local_hbm), custom_call_target="tpu_custom_call" | custom-call | flops 21743271936 | bytes 60000000 | tf_op jit(solution)/shard_map/left/pallas_call | solution.py:220
  106.8 0.0 copy-done.4
  106.8 0.6 broadcast_in_dim.10.x_ref
  107.4 12.3 %targets.1 = s32[16,8,128]{2,1,0:T(8,128)} custom-call(s32[16,8,128]{2,1,0:T(8,128)} %broadcast_in_dim.10.x_ref), custom_call_target="tpu_custom_call" | custom-call | bytes 300000000 | tf_op jit(solution)/shard_map/targets/pallas_call | solution.py:409
  119.8 0.2 convert_reduce_fusion.1
  120.0 0.9 fusion.9
  120.9 0.4 convert_reduce_fusion
  121.3 0.1 fusion.3
  121.4 0.2 select_reduce_fusion.from_ref
  121.6 0.0 copy-start.2
  121.6 0.7 pad_add_fusion.bucket_ref
  122.3 0.0 all-to-all-done.ghost_hbm
  122.3 17.8 %right0.1 = bf16[32,9,32,128]{3,2,1,0:T(8,128)(2,1)} custom-call(s32[4100]{0:T(1024)} %get-tuple-element.15.code_ref, s32[1025]{0:T(1024)} %get-tuple-element.16.group_ref, s32[4]{0:T(128)} %get-tuple-element.13.count_ref, s32[32]{0:T(128)} %pad_add_fusion.bucket_ref, bf16[2048,64,128]{2,1,0:T(8,128)(2,1)} %get-tuple-element.17.t_ref, ...), custom_call_target="tpu_custom_call" | custom-call | flops 21743271936 | bytes 30000000 | tf_op jit(solution)/shard_map/right0/pallas_call | solution.py:342
  140.1 0.0 copy-done.2
  140.1 7.7 %all-to-all-start.1 = ((bf16[16,576,128]{2,1,0:T(8,128)(2,1)}), bf16[16,576,128]{2,1,0:T(8,128)(2,1)}, u32[]{:S(2)}, u32[]{:S(2)}) async-start(bf16[16,576,128]{2,1,0:T(8,128)(2,1)} %bitcast.16), calls=%async_computation.1 | async-start | bytes 4718592 | tf_op jit(solution)/shard_map/all_to_all | solution.py:533
  147.8 26.4 %right1.1 = bf16[32,18,32,128]{3,2,1,0:T(8,128)(2,1)} custom-call(s32[4100]{0:T(1024)} %get-tuple-element.15.code_ref, s32[1025]{0:T(1024)} %get-tuple-element.16.group_ref, s32[4]{0:T(128)} %get-tuple-element.13.count_ref, s32[32]{0:T(128)} %pad_add_fusion.bucket_ref, bf16[2048,64,128]{2,1,0:T(8,128)(2,1)} %get-tuple-element.17.t_ref, ...), custom_call_target="tpu_custom_call" | custom-call | flops 21743271936 | bytes 30000000 | tf_op jit(solution)/shard_map/right1/pallas_call | solution.py:342
  174.2 69.1 %exchange.1 = bf16[16,1152,128]{2,1,0:T(8,128)(2,1)} custom-call(bf16[16,1152,128]{2,1,0:T(8,128)(2,1)} %bitcast.15), custom_call_target="tpu_custom_call" | custom-call | bytes 300000000 | tf_op jit(solution)/shard_map/exchange/pallas_call | solution.py:409
  243.3 0.0 all-to-all-done.1
  243.3 8.8 %place.1 = bf16[27,16,4096]{2,1,0:T(8,128)(2,1)} custom-call(s32[16]{0:T(128)} %copy-done.2, bf16[32,9,32,128]{3,2,1,0:T(8,128)(2,1)} %bitcast.6.refs_0_.refs_1_.refs_2_.refs_3_, bf16[32,9,32,128]{3,2,1,0:T(8,128)(2,1)} %bitcast.6.refs_0_.refs_1_.refs_2_.refs_3_, bf16[32,9,32,128]{3,2,1,0:T(8,128)(2,1)} %bitcast.6.refs_0_.refs_1_.refs_2_.refs_3_, ...), custom_call_target="tpu_custom_call" | custom-call | tf_op jit(solution)/shard_map/place/pallas_call | solution.py:472
  (8 shorter events, 0.1 us)
Async XLA Ops:
  9.8 11.0 %copy-start = (s32[96,27]{0,1:T(8,128)S(1)}, s32[96,27]{0,1:T(8,128)}, u32[]{:S(2)}) copy-start(s32[96,27]{0,1:T(8,128)} %param.12) | copy-start | bytes 31108
  9.8 11.0 %copy-start.3 = (s32[96]{0:T(128)S(1)}, s32[96]{0:T(128)}, u32[]{:S(2)}) copy-start(s32[96]{0:T(128)} %param.11) | copy-start | bytes 1156
  9.8 11.9 %copy-start.1 = (s32[96,27]{0,1:T(8,128)S(1)}, s32[96,27]{0,1:T(8,128)}, u32[]{:S(2)}) copy-start(s32[96,27]{0,1:T(8,128)} %param.9) | copy-start | bytes 31108
  9.8 112.5 %all-to-all-start = ((bf16[128,256,128]{2,1,0:T(8,128)(2,1)}), bf16[128,256,128]{2,1,0:T(8,128)(2,1)}, u32[]{:S(2)}, u32[]{:S(2)}) async-start(bf16[128,256,128]{2,1,0:T(8,128)(2,1)} %get-tuple-element.18), calls=%async_computation | async-start | bytes 16777216 | tf_op jit(solution)/shard_map/all_to_all | solution.py:519
  22.5 84.2 %copy-start.4 = (s32[16]{0:T(128)S(1)}, s32[16]{0:T(128)}, u32[]{:S(2)}) copy-start(s32[16]{0:T(128)} %param.13) | copy-start | bytes 196
  121.6 18.5 %copy-start.2 = (s32[16]{0:T(128)}, s32[16]{0:T(128)S(1)}, u32[]{:S(2)}) copy-start(s32[16]{0:T(128)S(1)} %select_reduce_fusion.from_ref) | copy-start | bytes 196
  140.1 103.2 %all-to-all-start.1 = ((bf16[16,576,128]{2,1,0:T(8,128)(2,1)}), bf16[16,576,128]{2,1,0:T(8,128)(2,1)}, u32[]{:S(2)}, u32[]{:S(2)}) async-start(bf16[16,576,128]{2,1,0:T(8,128)(2,1)} %bitcast.16), calls=%async_computation.1 | async-start | bytes 4718592 | tf_op jit(solution)/shard_map/all_to_all | solution.py:533

commit v5 on v4

--- a/solution.py
+++ b/solution.py
@@ -18,8 +18,11 @@
 NCL = NB // AGG
 PEERS = 128
 DEST = NCL * S
-PARTS = ((0, 9), (9, 18))
+PARTS = ((0, 8), (8, 19))
 SIDE = 4
+SHARES = 8
+PIECES = 4
+PAGE = 128
 GROUP = 4
 TILES = PEERS * Q // 2
 LOCAL = NB + 2
@@ -29,9 +32,9 @@
 PITCH = 72
 SPAN = Q // 2 * B
 NOTE = 8
-BATCH = 16
+BATCH = 32
 CHUNK_BITS = 7
-BATCH_BITS = 4
+BATCH_BITS = 5
 STEPS = GROUPS // CHUNK
 ROWS_STEP = 16
 F32 = jnp.float32
@@ -48,63 +51,66 @@
     )
 
 
-def pack_kernel(wanted, p_ref, send_ref, local_ref, wide):
-    step = pl.program_id(0)
-
-    @pl.when(step == 0)
-    def _():
-        low = low_lanes((ROWS_STEP, L))
-
-        def relayout(group, carry):
-            row = pl.multiple_of(group * ROWS_STEP, ROWS_STEP)
-            for m in range(B // 2):
-                both = p_ref[pl.ds(row, ROWS_STEP), pl.ds(m * L, L)].astype(F32)
-                turned = pltpu.roll(both, B, 1)
-                even = jnp.where(low, both, turned)
-                odd = jnp.where(low, turned, both)
-                wide[pl.ds(2 * m, ROWS_STEP, stride=PITCH), :] = even
-                wide[pl.ds(2 * m + 1, ROWS_STEP, stride=PITCH), :] = odd
-            for g in range(ROWS_STEP):
-                local_ref[row + g] = wide[pl.ds(g * PITCH, B), :].astype(BF16)
-            return carry
-
-        lax.fori_loop(0, NB // ROWS_STEP, relayout, 0)
-        zero = jnp.zeros((B, L), BF16)
-        local_ref[NB] = zero
-        local_ref[NB + 1] = zero
-
-    low = low_lanes((B, L))
-    per_step = send_ref.shape[0]
+def pack_kernel(wanted, p_ref, send_hbm, local_hbm, staged, blocks, wide, sems):
+    low = low_lanes((ROWS_STEP, L))
+
+    def relayout(group, carry):
+        row = pl.multiple_of(group * ROWS_STEP, ROWS_STEP)
+        for m in range(B // 2):
+            both = p_ref[pl.ds(row, ROWS_STEP), pl.ds(m * L, L)].astype(F32)
+            turned = pltpu.roll(both, B, 1)
+            even = jnp.where(low, both, turned)
+            odd = jnp.where(low, turned, both)
+            wide[pl.ds(2 * m, ROWS_STEP, stride=PITCH), :] = even
+            wide[pl.ds(2 * m + 1, ROWS_STEP, stride=PITCH), :] = odd
+        for g in range(ROWS_STEP):
+            blocks[row + g] = wide[pl.ds(g * PITCH, B), :].astype(BF16)
+        return carry
+
+    lax.fori_loop(0, NB // ROWS_STEP, relayout, 0)
+    zero = jnp.zeros((B, L), BF16)
+    blocks[NB] = zero
+    blocks[NB + 1] = zero
+    left_half = low_lanes((B, L))
+    share = PEERS // SHARES
 
     def fill(peer, carry):
         for u in range(Q // 2):
-            first = wanted[2 * u, step * per_step + peer]
-            second = wanted[2 * u + 1, step * per_step + peer]
+            first = wanted[2 * u, peer]
+            second = wanted[2 * u + 1, peer]
             first = jnp.where(first < 0, NB, first)
             second = jnp.where(second < 0, NB, second)
-            send_ref[peer, u * B : (u + 1) * B] = jnp.where(
-                low, local_ref[first], local_ref[second]
+            staged[peer, u * B : (u + 1) * B] = jnp.where(
+                left_half, blocks[first], blocks[second]
             )
         return carry
 
-    lax.fori_loop(0, per_step, fill, 0, unroll=2)
+    copies = []
+    for n in range(SHARES):
+        lax.fori_loop(n * share, (n + 1) * share, fill, 0, unroll=4)
+        part = pl.ds(n * share, share)
+        copies.append(pltpu.make_async_copy(staged.at[part], send_hbm.at[part], sems.at[n]))
+        copies[-1].start()
+    copies.append(pltpu.make_async_copy(blocks, local_hbm, sems.at[SHARES]))
+    copies[-1].start()
+    for copy in copies:
+        copy.wait()
 
 
 def pack(wanted, p_blocks):
-    per_step = PEERS // 8
     return pl.pallas_call(
         pack_kernel,
         grid_spec=pltpu.PrefetchScalarGridSpec(
             num_scalar_prefetch=1,
-            grid=(PEERS // per_step,),
-            in_specs=[
-                pl.BlockSpec((NB, B * B), lambda i, w: (0, 0)),
+            grid=(1,),
+            in_specs=[pl.BlockSpec((NB, B * B), lambda i, w: (0, 0))],
+            out_specs=[pl.BlockSpec(memory_space=pl.ANY)] * 2,
+            scratch_shapes=[
+                pltpu.VMEM((PEERS, SPAN, L), BF16),
+                pltpu.VMEM((LOCAL, B, L), BF16),
+                pltpu.VMEM((ROWS_STEP * PITCH, L), F32),
+                pltpu.SemaphoreType.DMA((SHARES + 1,)),
             ],
-            out_specs=[
-                pl.BlockSpec((per_step, SPAN, L), lambda i, w: (i, 0, 0)),
-                pl.BlockSpec((LOCAL, B, L), lambda i, w: (0, 0, 0)),
-            ],
-            scratch_shapes=[pltpu.VMEM((ROWS_STEP * PITCH, L), F32)],
         ),
         out_shape=[
             jax.ShapeDtypeStruct((PEERS, SPAN, L), BF16),
@@ -129,12 +135,15 @@
 
         lax.fori_loop(0, DEST, clear, 0, unroll=8)
 
-        def count(e, carry):
-            d = dest_in[e]
-            cursor[d] = cursor[d] + 1
-            return carry
-
-        lax.fori_loop(0, NB * K, count, 0, unroll=8)
+        def count_of(k, carry):
+            def count(row, carry):
+                d = dest_in[k, row]
+                cursor[d] = cursor[d] + 1
+                return carry
+
+            return lax.fori_loop(0, NB, count, carry, unroll=8)
+
+        lax.fori_loop(0, K, count_of, 0)
 
         def place(d, at):
             here = cursor[d]
@@ -176,12 +185,11 @@
     half = jnp.where(low, 0, 1)
 
     def insert(row, k, value, valid):
-        e = (step * ROWS_STEP + row) * K + k
-        d = dest_in[e]
+        d = dest_in[k, step * ROWS_STEP + row]
         at = cursor[d]
         cursor[d] = at + valid
         at = jnp.where(valid == 1, at, POSITIONS)
-        code_ref[at] = code_in[e]
+        code_ref[at] = code_in[k, step * ROWS_STEP + row]
         group_ref[at >> 2] = d
         tile = at >> 1
         held[tile] = jnp.where(half == (at & 1), value, held[tile].astype(F32)).astype(BF16)
@@ -211,9 +219,22 @@
 
     @pl.when(step == pl.num_programs(0) - 1)
     def _():
-        copy = pltpu.make_async_copy(held.at[pl.ds(0, 2 * GROUPS)], sorted_hbm, sem)
-        copy.start()
-        copy.wait()
+        used = (2 * count_ref[2 * len(PARTS) - 1] + PAGE - 1) >> 7
+
+        def page(n):
+            at = pl.ds(pl.multiple_of(n * PAGE, PAGE), PAGE)
+            return pltpu.make_async_copy(held.at[at], sorted_hbm.at[at], sem)
+
+        def begin(n, carry):
+            page(n).start()
+            return carry
+
+        def finish(n, carry):
+            page(n).wait()
+            return carry
+
+        lax.fori_loop(0, used, begin, 0)
+        lax.fori_loop(0, used, finish, 0)
 
 
 def left(dest, code, a_turned, local):
@@ -267,13 +288,20 @@
     @pl.when(step == 0)
     def _():
         mine = pltpu.make_async_copy(local_hbm, blocks.at[pl.ds(0, LOCAL)], sems.at[0])
-        others = pltpu.make_async_copy(
-            ghost_hbm,
-            blocks.at[pl.ds(LOCAL, TILES)].reshape(PEERS, SPAN, L),
-            sems.at[1],
-        )
+        piece = PEERS // PIECES
+        others = [
+            pltpu.make_async_copy(
+                ghost_hbm.at[pl.ds(n * piece, piece)],
+                blocks.at[pl.ds(LOCAL + n * piece * Q // 2, piece * Q // 2)].reshape(
+                    piece, SPAN, L
+                ),
+                sems.at[n + 1],
+            )
+            for n in range(PIECES)
+        ]
+        for copy in others:
+            copy.start()
         mine.start()
-        others.start()
         low = low_lanes((16, L))
         halves[0] = jnp.where(low, 1.0, 0.0).astype(BF16)
         halves[1] = jnp.where(low, 0.0, 1.0).astype(BF16)
@@ -285,7 +313,8 @@
 
         lax.fori_loop(0, width * NCL + 1, clear, 0, unroll=8)
         mine.wait()
-        others.wait()
+        for copy in others:
+            copy.wait()
 
     def batch(b, carry):
         for u in range(BATCH):
@@ -356,7 +385,7 @@
                 pltpu.VMEM((width * B, L), F32),
                 pltpu.VMEM((NCL, width, B // 2, L), BF16),
                 pltpu.VMEM((2, 16, L), BF16),
-                pltpu.SemaphoreType.DMA((2,)),
+                pltpu.SemaphoreType.DMA((PIECES + 1,)),
                 pltpu.SemaphoreType.DMA((NCL,)),
             ],
         ),
@@ -487,9 +516,9 @@
 
 
 def lists(a_source, agg_local, coarse_slot):
-    dest = (coarse_slot * NCL + agg_local[:, None]).reshape(-1)
+    dest = (coarse_slot * NCL + agg_local[:, None]).T
     ghost = a_source - NB + 2 * LOCAL
-    code = jnp.where(a_source < NB, 2 * a_source, ghost).reshape(-1)
+    code = jnp.where(a_source < NB, 2 * a_source, ghost).T
     return dest, code
 
 
@@ -522,13 +551,13 @@
     ordered, code, group, count = left(dest, code, a_blocks.transpose(1, 0, 2), local)
     tied, _ = lax.optimization_barrier((coarse_target, count))
     note = jnp.broadcast_to(jnp.pad(tied, (0, L - NCL)), (peers_y, NOTE, L))
-    targets = exchange(note, 1, "targets")[:, 0, :NCL]
-    origin = origins(targets, me)
+    targets = exchange(note, 1, "targets")
+    origin = origins(targets[:, 0, :NCL], me)
     bucket = jnp.concatenate([bucket, origin])
     arrived = []
     for part, (_, width) in enumerate(PARTS):
-        rows = right(part, code, group, count, bucket, ordered, local, ghost, peers_y)
-        rows = rows.reshape(peers_y, CCAP * width * B // 2, L)
+        formed = right(part, code, group, count, bucket, ordered, local, ghost, peers_y)
+        rows = formed.reshape(peers_y, CCAP * width * B // 2, L)
         if part == 0:
             rows = lax.all_to_all(rows, "py", split_axis=0, concat_axis=0, tiled=True)
         else:

time: 256 us -> 256 us (level); the launches traced: 252 us -> 255 us
  Pallas kernels: 228 us -> 233 us
    pallas_call x2, Pallas kernels: 81.4 us -> 91.4 us  [exchange(): pl.pallas_call(exchange_kernel, in_specs=[pl.BlockSpec(memory_space=pl.AN...]
    pallas_call x2, Pallas kernels: 44.3 us -> 41.3 us  [right(): pl.pallas_call(functools.partial(right_kernel, part), grid_spec=pltpu.Pre...]
  transfers between devices with their start and end apart: 2 -> 2, of which waited for: 0 -> 0; matrix products, arithmetic and copies ran while one was open for 2% -> 1% of each run, Pallas kernels for 76% -> 78%
where the time goes in v5:
time: 256 us; the launch traced here: 255 us
  Pallas kernels  233 us (91%)
  starting transfers between devices  18.7 us (7%)
  other arithmetic  3.13 us (1%)
    pallas_call x2, Pallas kernels, exchange(): pl.pallas_call(exchange_kernel, in_specs=[pl.BlockSpec(memory_space=pl.AN...  91.4 us
    pallas_call x1, Pallas kernels, left(): pl.pallas_call(left_kernel, grid_spec=pltpu.PrefetchScalarGridSpec(num_sc...  83.3 us
    pallas_call x2, Pallas kernels, right(): pl.pallas_call(functools.partial(right_kernel, part), grid_spec=pltpu.Pre...  41.3 us
    all_to_all x1, starting transfers between devices, body(): lax.all_to_all(sending, ('px', 'py'), split_axis=0, concat_axis=0, tiled=...  11 us
    pallas_call x1, Pallas kernels, place(): pl.pallas_call(place_kernel, grid_spec=pltpu.PrefetchScalarGridSpec(num_s...  8.79 us
    pallas_call x1, Pallas kernels, pack(): pl.pallas_call(pack_kernel, grid_spec=pltpu.PrefetchScalarGridSpec(num_sc...  8.04 us
    all_to_all x1, starting transfers between devices, body(): rows = lax.all_to_all(rows, 'py', split_axis=0, concat_axis=0, tiled=True)  7.69 us
  transfers between devices with their start and end apart: 2, of which 0 were waited for; matrix products, arithmetic and copies ran while one was open for 1% of the time, Pallas kernels for 78%

profile of v5, /device:TPU:2, one launch (start us, length us, event | category | flops | bytes accessed | tf_op | source)
XLA Modules:
  0.0 255.4 jit_solution(12977194969185016032)
XLA Ops:
  0.0 8.0 %pack.1 = (bf16[128,256,128]{2,1,0:T(8,128)(2,1)}, bf16[98,64,128]{2,1,0:T(8,128)(2,1)}) custom-call(s32[8,128]{1,0:T(8,128)} %bitcast.24, bf16[96,4096]{1,0:T(8,128)(2,1)} %p_ref.1), custom_call_target="tpu_custom_call" | custom-call | tf_op jit(solution)/shard_map/pack/pallas_call | solution.py:101
  8.0 0.0 copy-start
  8.1 0.0 copy-start.1
  8.1 0.0 copy-start.3
  8.1 11.0 %all-to-all-start = ((bf16[128,256,128]{2,1,0:T(8,128)(2,1)}), bf16[128,256,128]{2,1,0:T(8,128)(2,1)}, u32[]{:S(2)}, u32[]{:S(2)}) async-start(bf16[128,256,128]{2,1,0:T(8,128)(2,1)} %get-tuple-element.18), calls=%async_computation | async-start | bytes 16777216 | tf_op jit(solution)/shard_map/all_to_all | solution.py:548
  19.1 0.0 copy-done
  19.1 0.0 copy-done.1
  19.1 0.0 copy-done.3
  19.1 0.6 select_bitcast_fusion
  19.7 0.0 copy-start.4
  19.7 83.3 %left.1 = (bf16[2048,64,128]{2,1,0:T(8,128)(2,1)}, s32[4100]{0:T(1024)}, s32[1025]{0:T(1024)}, s32[4]{0:T(128)}) custom-call(s32[27,96]{1,0:T(8,128)} %get-tuple-element.24.dest_in, s32[27,96]{1,0:T(8,128)} %get-tuple-element.23.code_in, bf16[27,96,4096]{2,1,0:T(8,128)(2,1)} %bitcast.25, bf16[98,64,128]{2,1,0:T(8,128)(2,1)} %get-tuple-element.12.p_ref.local_hbm), custom_call_target="tpu_custom_call" | custom-call | flops 21743271936 | bytes 60000000 | tf_op jit(solution)/shard_map/left/pallas_call | solution.py:241
  103.0 0.0 copy-done.4
  103.0 0.6 broadcast_in_dim.10.x_ref
  103.7 14.4 %targets.1 = s32[16,8,128]{2,1,0:T(8,128)} custom-call(s32[16,8,128]{2,1,0:T(8,128)} %broadcast_in_dim.10.x_ref), custom_call_target="tpu_custom_call" | custom-call | bytes 300000000 | tf_op jit(solution)/shard_map/targets/pallas_call | solution.py:438
  118.1 0.2 convert_reduce_fusion.1
  118.3 0.9 fusion.9
  119.2 0.4 convert_reduce_fusion
  119.7 0.1 fusion.3
  119.7 0.2 select_reduce_fusion.from_ref
  119.9 0.0 copy-start.2
  119.9 0.7 pad_add_fusion.bucket_ref
  120.6 0.0 all-to-all-done.ghost_hbm
  120.6 15.7 %right0.1 = bf16[32,8,32,128]{3,2,1,0:T(8,128)(2,1)} custom-call(s32[4100]{0:T(1024)} %get-tuple-element.15.code_ref, s32[1025]{0:T(1024)} %get-tuple-element.16.group_ref, s32[4]{0:T(128)} %get-tuple-element.13.count_ref, s32[32]{0:T(128)} %pad_add_fusion.bucket_ref, bf16[2048,64,128]{2,1,0:T(8,128)(2,1)} %get-tuple-element.17.t_ref, ...), custom_call_target="tpu_custom_call" | custom-call | flops 21743271936 | bytes 30000000 | tf_op jit(solution)/shard_map/right0/pallas_call | solution.py:371
  136.4 0.0 copy-done.2
  136.4 7.7 %all-to-all-start.1 = ((bf16[16,512,128]{2,1,0:T(8,128)(2,1)}), bf16[16,512,128]{2,1,0:T(8,128)(2,1)}, u32[]{:S(2)}, u32[]{:S(2)}) async-start(bf16[16,512,128]{2,1,0:T(8,128)(2,1)} %bitcast.20), calls=%async_computation.1 | async-start | bytes 4194304 | tf_op jit(solution)/shard_map/all_to_all | solution.py:562
  144.1 25.6 %right1.1 = bf16[32,19,32,128]{3,2,1,0:T(8,128)(2,1)} custom-call(s32[4100]{0:T(1024)} %get-tuple-element.15.code_ref, s32[1025]{0:T(1024)} %get-tuple-element.16.group_ref, s32[4]{0:T(128)} %get-tuple-element.13.count_ref, s32[32]{0:T(128)} %pad_add_fusion.bucket_ref, bf16[2048,64,128]{2,1,0:T(8,128)(2,1)} %get-tuple-element.17.t_ref, ...), custom_call_target="tpu_custom_call" | custom-call | flops 21743271936 | bytes 30000000 | tf_op jit(solution)/shard_map/right1/pallas_call | solution.py:371
  169.6 77.0 %exchange.1 = bf16[16,1216,128]{2,1,0:T(8,128)(2,1)} custom-call(bf16[16,1216,128]{2,1,0:T(8,128)(2,1)} %bitcast.19), custom_call_target="tpu_custom_call" | custom-call | bytes 300000000 | tf_op jit(solution)/shard_map/exchange/pallas_call | solution.py:438
  246.7 0.0 all-to-all-done.1
  246.7 8.8 %place.1 = bf16[27,16,4096]{2,1,0:T(8,128)(2,1)} custom-call(s32[16]{0:T(128)} %copy-done.2, bf16[32,8,32,128]{3,2,1,0:T(8,128)(2,1)} %bitcast.8.refs_0_.refs_1_.refs_2_.refs_3_, bf16[32,8,32,128]{3,2,1,0:T(8,128)(2,1)} %bitcast.8.refs_0_.refs_1_.refs_2_.refs_3_, bf16[32,8,32,128]{3,2,1,0:T(8,128)(2,1)} %bitcast.8.refs_0_.refs_1_.refs_2_.refs_3_, ...), custom_call_target="tpu_custom_call" | custom-call | tf_op jit(solution)/shard_map/place/pallas_call | solution.py:501
  (7 shorter events, 0.1 us)
Async XLA Ops:
  8.0 11.0 %copy-start = (s32[96,27]{0,1:T(8,128)S(1)}, s32[96,27]{0,1:T(8,128)}, u32[]{:S(2)}) copy-start(s32[96,27]{0,1:T(8,128)} %param.9) | copy-start | bytes 31108
  8.1 11.0 %copy-start.1 = (s32[96,27]{0,1:T(8,128)S(1)}, s32[96,27]{0,1:T(8,128)}, u32[]{:S(2)}) copy-start(s32[96,27]{0,1:T(8,128)} %param.12) | copy-start | bytes 31108
  8.1 11.0 %copy-start.3 = (s32[96]{0:T(128)S(1)}, s32[96]{0:T(128)}, u32[]{:S(2)}) copy-start(s32[96]{0:T(128)} %param.11) | copy-start | bytes 1156
  8.1 112.5 %all-to-all-start = ((bf16[128,256,128]{2,1,0:T(8,128)(2,1)}), bf16[128,256,128]{2,1,0:T(8,128)(2,1)}, u32[]{:S(2)}, u32[]{:S(2)}) async-start(bf16[128,256,128]{2,1,0:T(8,128)(2,1)} %get-tuple-element.18), calls=%async_computation | async-start | bytes 16777216 | tf_op jit(solution)/shard_map/all_to_all | solution.py:548
  19.7 83.3 %copy-start.4 = (s32[16]{0:T(128)S(1)}, s32[16]{0:T(128)}, u32[]{:S(2)}) copy-start(s32[16]{0:T(128)} %param.13) | copy-start | bytes 196
  119.9 16.4 %copy-start.2 = (s32[16]{0:T(128)}, s32[16]{0:T(128)S(1)}, u32[]{:S(2)}) copy-start(s32[16]{0:T(128)S(1)} %select_reduce_fusion.from_ref) | copy-start | bytes 196
  136.4 110.3 %all-to-all-start.1 = ((bf16[16,512,128]{2,1,0:T(8,128)(2,1)}), bf16[16,512,128]{2,1,0:T(8,128)(2,1)}, u32[]{:S(2)}, u32[]{:S(2)}) async-start(bf16[16,512,128]{2,1,0:T(8,128)(2,1)} %bitcast.20), calls=%async_computation.1 | async-start | bytes 4194304 | tf_op jit(solution)/shard_map/all_to_all | solution.py:562

commit v6 on v5

--- a/solution.py
+++ b/solution.py
@@ -18,7 +18,8 @@
 NCL = NB // AGG
 PEERS = 128
 DEST = NCL * S
-PARTS = ((0, 8), (8, 19))
+PARTS = ((0, 9), (9, 18))
+COUNTERS = 4
 SIDE = 4
 SHARES = 8
 PIECES = 4
@@ -123,30 +124,33 @@
 
 def left_kernel(
     dest_in, code_in, a_ref, p_ref, sorted_hbm, code_ref, group_ref, count_ref,
-    held, wide, turned_p, cursor, sem,
+    held, wide, turned_p, cursor, *rest,
 ):
+    counters, sem = (cursor, *rest[:-1]), rest[-1]
     step = pl.program_id(0)
 
     @pl.when(step == 0)
     def _():
         def clear(d, carry):
-            cursor[d] = 0
+            for counter in counters:
+                counter[d] = 0
             return carry
 
         lax.fori_loop(0, DEST, clear, 0, unroll=8)
 
         def count_of(k, carry):
             def count(row, carry):
-                d = dest_in[k, row]
-                cursor[d] = cursor[d] + 1
+                for n, counter in enumerate(counters):
+                    d = dest_in[k, n * (NB // COUNTERS) + row]
+                    counter[d] = counter[d] + 1
                 return carry
 
-            return lax.fori_loop(0, NB, count, carry, unroll=8)
+            return lax.fori_loop(0, NB // COUNTERS, count, carry, unroll=8)
 
         lax.fori_loop(0, K, count_of, 0)
 
         def place(d, at):
-            here = cursor[d]
+            here = sum(counter[d] for counter in counters)
             cursor[d] = at
             return at + ((here + GROUP - 1) & -GROUP)
 
@@ -257,7 +261,7 @@
                 pltpu.VMEM((2 * GROUPS + 1, B, L), BF16),
                 pltpu.VMEM((ROWS_STEP * PITCH, L), F32),
                 pltpu.VMEM((ROWS_STEP, B, B), BF16),
-                pltpu.SMEM((DEST,), jnp.int32),
+                *[pltpu.SMEM((DEST,), jnp.int32) for _ in range(COUNTERS)],
                 pltpu.SemaphoreType.DMA,
             ],
         ),

time: 256 us -> 252 us (0.984)
  Pallas kernels: 233 us -> 227 us
    pallas_call x1, Pallas kernels: 83.3 us -> 79.7 us  [left(): pl.pallas_call(left_kernel, grid_spec=pltpu.PrefetchScalarGridSpec(num_sc...]
  transfers between devices with their start and end apart: 2 -> 2, of which waited for: 0 -> 0; matrix products, arithmetic and copies ran while one was open for 1% -> 2% of each run, Pallas kernels for 78% -> 78%
where the time goes in v6:
time: 252 us; the launch traced here: 250 us
  Pallas kernels  227 us (90%)
  starting transfers between devices  18.7 us (7%)
  other arithmetic  3.13 us (1%)
    pallas_call x2, Pallas kernels, exchange(): pl.pallas_call(exchange_kernel, in_specs=[pl.BlockSpec(memory_space=pl.AN...  89.6 us
    pallas_call x1, Pallas kernels, left(): pl.pallas_call(left_kernel, grid_spec=pltpu.PrefetchScalarGridSpec(num_sc...  79.7 us
    pallas_call x2, Pallas kernels, right(): pl.pallas_call(functools.partial(right_kernel, part), grid_spec=pltpu.Pre...  41.3 us
    all_to_all x1, starting transfers between devices, body(): lax.all_to_all(sending, ('px', 'py'), split_axis=0, concat_axis=0, tiled=...  11 us
    pallas_call x1, Pallas kernels, place(): pl.pallas_call(place_kernel, grid_spec=pltpu.PrefetchScalarGridSpec(num_s...  8.82 us
    pallas_call x1, Pallas kernels, pack(): pl.pallas_call(pack_kernel, grid_spec=pltpu.PrefetchScalarGridSpec(num_sc...  8.04 us
    all_to_all x1, starting transfers between devices, body(): rows = lax.all_to_all(rows, 'py', split_axis=0, concat_axis=0, tiled=True)  7.67 us
  transfers between devices with their start and end apart: 2, of which 0 were waited for; matrix products, arithmetic and copies ran while one was open for 2% of the time, Pallas kernels for 78%

profile of v6, /device:TPU:2, one launch (start us, length us, event | category | flops | bytes accessed | tf_op | source)
XLA Modules:
  0.0 250.1 jit_solution(5360695386297460329)
XLA Ops:
  0.0 8.0 %pack.1 = (bf16[128,256,128]{2,1,0:T(8,128)(2,1)}, bf16[98,64,128]{2,1,0:T(8,128)(2,1)}) custom-call(s32[8,128]{1,0:T(8,128)} %bitcast.24, bf16[96,4096]{1,0:T(8,128)(2,1)} %p_ref.1), custom_call_target="tpu_custom_call" | custom-call | tf_op jit(solution)/shard_map/pack/pallas_call | solution.py:102
  8.0 0.0 copy-start
  8.1 0.0 copy-start.1
  8.1 0.0 copy-start.3
  8.1 11.0 %all-to-all-start = ((bf16[128,256,128]{2,1,0:T(8,128)(2,1)}), bf16[128,256,128]{2,1,0:T(8,128)(2,1)}, u32[]{:S(2)}, u32[]{:S(2)}) async-start(bf16[128,256,128]{2,1,0:T(8,128)(2,1)} %get-tuple-element.18), calls=%async_computation | async-start | bytes 16777216 | tf_op jit(solution)/shard_map/all_to_all | solution.py:552
  19.1 0.0 copy-done
  19.1 0.0 copy-done.1
  19.1 0.0 copy-done.3
  19.1 0.6 select_bitcast_fusion
  19.7 0.0 copy-start.4
  19.7 79.7 %left.1 = (bf16[2048,64,128]{2,1,0:T(8,128)(2,1)}, s32[4100]{0:T(1024)}, s32[1025]{0:T(1024)}, s32[4]{0:T(128)}) custom-call(s32[27,96]{1,0:T(8,128)} %get-tuple-element.24.dest_in, s32[27,96]{1,0:T(8,128)} %get-tuple-element.23.code_in, bf16[27,96,4096]{2,1,0:T(8,128)(2,1)} %bitcast.25, bf16[98,64,128]{2,1,0:T(8,128)(2,1)} %get-tuple-element.12.p_ref.local_hbm), custom_call_target="tpu_custom_call" | custom-call | flops 21743271936 | bytes 60000000 | tf_op jit(solution)/shard_map/left/pallas_call | solution.py:245
  99.5 0.0 copy-done.4
  99.5 0.6 broadcast_in_dim.10.x_ref
  100.1 17.9 %targets.1 = s32[16,8,128]{2,1,0:T(8,128)} custom-call(s32[16,8,128]{2,1,0:T(8,128)} %broadcast_in_dim.10.x_ref), custom_call_target="tpu_custom_call" | custom-call | bytes 300000000 | tf_op jit(solution)/shard_map/targets/pallas_call | solution.py:442
  118.1 0.2 convert_reduce_fusion.1
  118.3 0.9 fusion.9
  119.2 0.4 convert_reduce_fusion
  119.7 0.1 fusion.3
  119.7 0.2 select_reduce_fusion.from_ref
  119.9 0.0 copy-start.2
  119.9 0.7 pad_add_fusion.bucket_ref
  120.6 0.0 all-to-all-done.ghost_hbm
  120.6 16.6 %right0.1 = bf16[32,9,32,128]{3,2,1,0:T(8,128)(2,1)} custom-call(s32[4100]{0:T(1024)} %get-tuple-element.15.code_ref, s32[1025]{0:T(1024)} %get-tuple-element.16.group_ref, s32[4]{0:T(128)} %get-tuple-element.13.count_ref, s32[32]{0:T(128)} %pad_add_fusion.bucket_ref, bf16[2048,64,128]{2,1,0:T(8,128)(2,1)} %get-tuple-element.17.t_ref, ...), custom_call_target="tpu_custom_call" | custom-call | flops 21743271936 | bytes 30000000 | tf_op jit(solution)/shard_map/right0/pallas_call | solution.py:375
  137.2 0.0 copy-done.2
  137.3 7.7 %all-to-all-start.1 = ((bf16[16,576,128]{2,1,0:T(8,128)(2,1)}), bf16[16,576,128]{2,1,0:T(8,128)(2,1)}, u32[]{:S(2)}, u32[]{:S(2)}) async-start(bf16[16,576,128]{2,1,0:T(8,128)(2,1)} %bitcast.20), calls=%async_computation.1 | async-start | bytes 4718592 | tf_op jit(solution)/shard_map/all_to_all | solution.py:566
  144.9 24.7 %right1.1 = bf16[32,18,32,128]{3,2,1,0:T(8,128)(2,1)} custom-call(s32[4100]{0:T(1024)} %get-tuple-element.15.code_ref, s32[1025]{0:T(1024)} %get-tuple-element.16.group_ref, s32[4]{0:T(128)} %get-tuple-element.13.count_ref, s32[32]{0:T(128)} %pad_add_fusion.bucket_ref, bf16[2048,64,128]{2,1,0:T(8,128)(2,1)} %get-tuple-element.17.t_ref, ...), custom_call_target="tpu_custom_call" | custom-call | flops 21743271936 | bytes 30000000 | tf_op jit(solution)/shard_map/right1/pallas_call | solution.py:375
  169.6 71.7 %exchange.1 = bf16[16,1152,128]{2,1,0:T(8,128)(2,1)} custom-call(bf16[16,1152,128]{2,1,0:T(8,128)(2,1)} %bitcast.19), custom_call_target="tpu_custom_call" | custom-call | bytes 300000000 | tf_op jit(solution)/shard_map/exchange/pallas_call | solution.py:442
  241.3 0.0 all-to-all-done.1
  241.3 8.8 %place.1 = bf16[27,16,4096]{2,1,0:T(8,128)(2,1)} custom-call(s32[16]{0:T(128)} %copy-done.2, bf16[32,9,32,128]{3,2,1,0:T(8,128)(2,1)} %bitcast.8.refs_0_.refs_1_.refs_2_.refs_3_, bf16[32,9,32,128]{3,2,1,0:T(8,128)(2,1)} %bitcast.8.refs_0_.refs_1_.refs_2_.refs_3_, bf16[32,9,32,128]{3,2,1,0:T(8,128)(2,1)} %bitcast.8.refs_0_.refs_1_.refs_2_.refs_3_, ...), custom_call_target="tpu_custom_call" | custom-call | tf_op jit(solution)/shard_map/place/pallas_call | solution.py:505
  (7 shorter events, 0.1 us)
Async XLA Ops:
  8.0 11.0 %copy-start = (s32[96,27]{0,1:T(8,128)S(1)}, s32[96,27]{0,1:T(8,128)}, u32[]{:S(2)}) copy-start(s32[96,27]{0,1:T(8,128)} %param.9) | copy-start | bytes 31108
  8.1 11.0 %copy-start.1 = (s32[96,27]{0,1:T(8,128)S(1)}, s32[96,27]{0,1:T(8,128)}, u32[]{:S(2)}) copy-start(s32[96,27]{0,1:T(8,128)} %param.12) | copy-start | bytes 31108
  8.1 11.0 %copy-start.3 = (s32[96]{0:T(128)S(1)}, s32[96]{0:T(128)}, u32[]{:S(2)}) copy-start(s32[96]{0:T(128)} %param.11) | copy-start | bytes 1156
  8.1 112.5 %all-to-all-start = ((bf16[128,256,128]{2,1,0:T(8,128)(2,1)}), bf16[128,256,128]{2,1,0:T(8,128)(2,1)}, u32[]{:S(2)}, u32[]{:S(2)}) async-start(bf16[128,256,128]{2,1,0:T(8,128)(2,1)} %get-tuple-element.18), calls=%async_computation | async-start | bytes 16777216 | tf_op jit(solution)/shard_map/all_to_all | solution.py:552
  19.7 79.7 %copy-start.4 = (s32[16]{0:T(128)S(1)}, s32[16]{0:T(128)}, u32[]{:S(2)}) copy-start(s32[16]{0:T(128)} %param.13) | copy-start | bytes 196
  119.9 17.3 %copy-start.2 = (s32[16]{0:T(128)}, s32[16]{0:T(128)S(1)}, u32[]{:S(2)}) copy-start(s32[16]{0:T(128)S(1)} %select_reduce_fusion.from_ref) | copy-start | bytes 196
  137.3 104.0 %all-to-all-start.1 = ((bf16[16,576,128]{2,1,0:T(8,128)(2,1)}), bf16[16,576,128]{2,1,0:T(8,128)(2,1)}, u32[]{:S(2)}, u32[]{:S(2)}) async-start(bf16[16,576,128]{2,1,0:T(8,128)(2,1)} %bitcast.20), calls=%async_computation.1 | async-start | bytes 4718592 | tf_op jit(solution)/shard_map/all_to_all | solution.py:566
